TPU v7x, 32 devices: a whole 2x2x4 slice. The times are simulated.
32 devices in a mesh: dp: 8 (over z, y), tensor: 4 (over x, core).
Axes of the slice: x: 2, y: 2, z: 4, core: 2. Of those that a mesh axis runs over, the one named last changes fastest.
Arguments:
- block_input: bfloat16 [8192, 2048], P(('dp', 'tensor')), may hold values from -6 to 6
- cotangent: bfloat16 [8192, 2048], P(('dp', 'tensor')), may hold values from -6 to 6
- ln1_gain: float32 [2048], replicated, may hold values from 0.5 to 1.5
- ln1_bias: float32 [2048], replicated, may hold values from -1.5 to 1.5
- w_query: bfloat16 [2048, 2048], P('dp', 'tensor'), may hold values from -0.125 to 0.125
- q_bias: float32 [2048], replicated, may hold values from -1.5 to 1.5
- w_key: bfloat16 [2048, 2048], P('dp', 'tensor'), may hold values from -0.125 to 0.125
- k_bias: float32 [512], replicated, may hold values from -1.5 to 1.5
- w_value: bfloat16 [2048, 2048], P('dp', 'tensor'), may hold values from -0.125 to 0.125
- v_bias: float32 [2048], replicated, may hold values from -1.5 to 1.5
- w_out: bfloat16 [2048, 2048], P('dp', 'tensor'), may hold values from -0.375 to 0.375
- ln2_gain: float32 [2048], replicated, may hold values from 0.5 to 1.5
- ln2_bias: float32 [2048], replicated, may hold values from -1.5 to 1.5
- w_gate: bfloat16 [2048, 5632], P('dp', 'tensor'), may hold values from -0.125 to 0.125
- w_up: bfloat16 [2048, 5632], P('dp', 'tensor'), may hold values from -0.125 to 0.125
- w_down: bfloat16 [2048, 5632], P('dp', 'tensor'), may hold values from -0.15625 to 0.15625
Outputs:
- block_output: bfloat16 [8192, 2048], P(('dp', 'tensor'))
- input_grad: float32 [8192, 2048], P(('dp', 'tensor'))
- ln1_gain_grad: float32 [2048], replicated
- ln1_bias_grad: float32 [2048], replicated
- w_query_grad: float32 [2048, 2048], P('dp', 'tensor')
- q_bias_grad: float32 [2048], replicated
- w_key_grad: float32 [2048, 2048], P('dp', 'tensor')
- k_bias_grad: float32 [512], replicated
- w_value_grad: float32 [2048, 2048], P('dp', 'tensor')
- v_bias_grad: float32 [2048], replicated
- w_out_grad: float32 [2048, 2048], P('dp', 'tensor')
- ln2_gain_grad: float32 [2048], replicated
- ln2_bias_grad: float32 [2048], replicated
- w_gate_grad: float32 [2048, 5632], P('dp', 'tensor')
- w_up_grad: float32 [2048, 5632], P('dp', 'tensor')
- w_down_grad: float32 [2048, 5632], P('dp', 'tensor')
All inputs are finite; a program needn't handle non-finite values.
Results may differ from a plain program's by a relative error of at most 0.019.
Values may be sent and summed in bfloat16 or wider, within the bound.
No kernel may reach another device: no remote copies, remote signals or barrier semaphores. Data moves between devices by JAX's collectives and lax.ppermute only.
A program may use at most 192 MiB of HBM per device.

v0:
```python
import functools

import jax
import jax.numpy as jnp
from jax import lax
from jax.experimental import pallas as pl
from jax.experimental.pallas import tpu as pltpu
from jax.sharding import PartitionSpec as P

HEAD = 64
ROT = 16
EPS = 1e-05
LITTLE = pl.CostEstimate(flops=0, bytes_accessed=0, transcendentals=0)
BF = jnp.bfloat16
F32 = jnp.float32


def dot(left, right):
    return jnp.dot(left, right, preferred_element_type=F32)


def times_transposed(left, right):
    return lax.dot_general(left, right, (((1,), (1,)), ((), ())), preferred_element_type=F32)


def over_rows(left, right):
    return lax.dot_general(left, right, (((0,), (0,)), ((), ())), preferred_element_type=F32)


def dot_nt(left, right):
    return times_transposed(left, right)


def after(value, *others):
    return lax.optimization_barrier((value, *others))[0]


def all_after(values, *others):
    return lax.optimization_barrier((*values, *others))[: len(values)]


def head_mask(shape, head):
    lane = lax.broadcasted_iota(jnp.int32, shape, len(shape) - 1)
    return (lane >= head * HEAD) & (lane < (head + 1) * HEAD)


def turn(values, cosine, sine):
    half = ROT // 2
    parts = []
    for start in range(0, values.shape[1], 128):
        v = values[:, start : start + 128]
        lane = lax.broadcasted_iota(jnp.int32, v.shape, 1) % HEAD
        other = jnp.where(lane < half, pltpu.roll(v, 128 - half, 1), pltpu.roll(v, half, 1))
        parts.append(v * cosine + other * sine)
    return jnp.concatenate(parts, 1)


def turn_tables(place):
    half = ROT // 2
    frequency = 10000.0 ** (-2.0 * jnp.arange(half, dtype=F32) / ROT)
    angles = place.astype(F32)[:, None] * frequency[None, :]
    cosine, sine = jnp.cos(angles), jnp.sin(angles)
    rest = jnp.ones((place.shape[0], HEAD - ROT), F32)
    one = jnp.concatenate([cosine, cosine, rest], 1)
    two = jnp.concatenate([-sine, sine, 0.0 * rest], 1)
    return jnp.concatenate([one, one], 1), jnp.concatenate([two, two], 1)


def attend_kernel(me, pre, shift, cosine, sine, qkv, context, log_total):
    slots, rows, wide = pre.shape[1:]
    cols = wide // 3
    heads = cols // HEAD
    for s in range(slots):
        for part in range(3):
            at = slice(part * cols, (part + 1) * cols)
            v = pre[0, s, :, at] + shift[:, at]
            if part < 2:
                v = turn(v, cosine[s], sine[s])
            qkv[0, s, :, at] = v.astype(BF)
    where = [jnp.bitwise_xor(me[0], b) for b in range(slots)]
    key_row = lax.broadcasted_iota(jnp.int32, (rows, rows), 1)
    query_row = lax.broadcasted_iota(jnp.int32, (rows, rows), 0)
    lane = lax.broadcasted_iota(jnp.int32, (rows, 128), 1)
    for i in range(slots):
        query = qkv[0, where[i], :, :cols] * jnp.asarray(0.125, BF)
        total_context = jnp.zeros((rows, cols), F32)
        logs = jnp.zeros((rows, 128), F32)
        for h in range(heads):
            mask = head_mask((rows, cols), h)
            one = jnp.where(mask, query, jnp.zeros_like(query))
            scores = [dot_nt(one, qkv[0, where[j], :, cols : 2 * cols]) for j in range(i + 1)]
            scores[i] = jnp.where(key_row <= query_row, scores[i], -1e30)
            top = jnp.max(functools.reduce(jnp.maximum, scores), 1, keepdims=True)
            weights = [jnp.exp(v - top) for v in scores]
            total = jnp.sum(functools.reduce(jnp.add, weights), 1, keepdims=True)
            mixed = functools.reduce(
                jnp.add,
                [dot(w.astype(BF), qkv[0, where[j], :, 2 * cols :]) for j, w in enumerate(weights)],
            )
            total_context = jnp.where(mask, mixed * (1.0 / total), total_context)
            logs = jnp.where(lane == h, top + jnp.log(total), logs)
        context[0, where[i]] = total_context.astype(BF)
        log_total[0, i] = logs.T[:8]


def attend(me, pre, shift, cosine, sine):
    two, slots, rows, wide = pre.shape
    cols = wide // 3

    def seq(*dims):
        return pl.BlockSpec((1, *dims), lambda i, me: (i,) + (0,) * len(dims))

    def whole(*dims):
        return pl.BlockSpec(dims, lambda i, me: (0,) * len(dims))

    pairs = two * slots * (slots + 1) // 2 * (cols // HEAD)
    return pl.pallas_call(
        attend_kernel,
        grid_spec=pltpu.PrefetchScalarGridSpec(
            num_scalar_prefetch=1,
            grid=(two,),
            in_specs=[seq(slots, rows, wide), whole(1, wide), whole(slots, rows, 128), whole(slots, rows, 128)],
            out_specs=[seq(slots, rows, wide), seq(slots, rows, cols), seq(slots, 8, rows)],
        ),
        out_shape=[
            jax.ShapeDtypeStruct((two, slots, rows, wide), BF),
            jax.ShapeDtypeStruct((two, slots, rows, cols), BF),
            jax.ShapeDtypeStruct((two, slots, 8, rows), F32),
        ],
        compiler_params=pltpu.CompilerParams(vmem_limit_bytes=40 * 2**20),
        cost_estimate=LITTLE,
        name="attend",
    )(me, pre, shift, cosine, sine)


def attend_back_kernel(
    me, qkv, context, d_context, log_total, cosine, sine, d_qkv, sums, query, upstream, d_query, delta
):
    slots, rows, wide = qkv.shape[1:]
    cols = wide // 3
    heads = cols // HEAD
    where = [jnp.bitwise_xor(me[0], b) for b in range(slots)]
    row = lax.broadcasted_iota(jnp.int32, (8, cols), 0)
    picks = jnp.zeros((8, cols), F32)
    for h in range(heads):
        picks = jnp.where((row == h) & head_mask((8, cols), h), 1.0, picks)
    picks = picks.astype(BF)
    for i in range(slots):
        at = slice(i * rows, (i + 1) * rows)
        query[at] = qkv[0, where[i], :, :cols] * jnp.asarray(0.125, BF)
        up = d_context[0, where[i]]
        upstream[at] = up
        product = up.astype(F32) * context[0, where[i]].astype(F32)
        high = product.astype(BF)
        low = (product - high.astype(F32)).astype(BF)
        delta[:, at] = dot_nt(picks, high) + dot_nt(picks, low)
    key_row = lax.broadcasted_iota(jnp.int32, (rows, rows), 0)
    query_row = lax.broadcasted_iota(jnp.int32, (rows, rows), 1)
    total_sums = [jnp.zeros((1, cols), F32) for _ in range(3)]
    for j in range(slots):
        key = qkv[0, where[j], :, cols : 2 * cols]
        value = qkv[0, where[j], :, 2 * cols :]
        d_key = jnp.zeros((rows, cols), F32)
        d_value = jnp.zeros((rows, cols), F32)
        for h in range(heads):
            mask = head_mask((rows, cols), h)
            key_one = jnp.where(mask, key, jnp.zeros_like(key))
            value_one = jnp.where(mask, value, jnp.zeros_like(value))
            for i in range(j, slots):
                at = slice(i * rows, (i + 1) * rows)
                query_here, up_here = query[at], upstream[at]
                scores = dot_nt(key_one, query_here)
                if i == j:
                    scores = jnp.where(key_row <= query_row, scores, -1e30)
                probs = jnp.exp(scores - log_total[0, i, h : h + 1, :])
                d_probs = dot_nt(value_one, up_here)
                d_scores = (probs * (d_probs - delta[h : h + 1, at])).astype(BF)
                d_value = jnp.where(mask, d_value + dot(probs.astype(BF), up_here), d_value)
                d_key = jnp.where(mask, d_key + dot(d_scores, query_here), d_key)
                d_query_part = over_rows(d_scores, key_one)
                if j == 0 and h == 0:
                    d_query[at] = d_query_part
                else:
                    d_query[at] += d_query_part
        s = where[j]
        d_key_low = turn(d_key, cosine[s], -sine[s]).astype(BF)
        d_value_low = d_value.astype(BF)
        d_qkv[0, s, :, cols : 2 * cols] = d_key_low
        d_qkv[0, s, :, 2 * cols :] = d_value_low
        d_query_low = turn(d_query[j * rows : (j + 1) * rows] * 0.125, cosine[s], -sine[s]).astype(BF)
        d_qkv[0, s, :, :cols] = d_query_low
        for part, v in enumerate((d_query_low, d_key_low, d_value_low)):
            total_sums[part] += jnp.sum(v.astype(F32), 0, keepdims=True)
    sums[0] = jnp.concatenate(total_sums, 1)


def attend_back(me, qkv, context, d_context, log_total, cosine, sine):
    two, slots, rows, wide = qkv.shape
    cols = wide // 3

    def seq(*dims):
        return pl.BlockSpec((1, *dims), lambda i, me: (i,) + (0,) * len(dims))

    def whole(*dims):
        return pl.BlockSpec(dims, lambda i, me: (0,) * len(dims))

    return pl.pallas_call(
        attend_back_kernel,
        grid_spec=pltpu.PrefetchScalarGridSpec(
            num_scalar_prefetch=1,
            grid=(two,),
            in_specs=[
                seq(slots, rows, wide),
                seq(slots, rows, cols),
                seq(slots, rows, cols),
                seq(slots, 8, rows),
                whole(slots, rows, 128),
                whole(slots, rows, 128),
            ],
            out_specs=[seq(slots, rows, wide), seq(1, wide)],
            scratch_shapes=[
                pltpu.VMEM((slots * rows, cols), BF),
                pltpu.VMEM((slots * rows, cols), BF),
                pltpu.VMEM((slots * rows, cols), F32),
                pltpu.VMEM((8, slots * rows), F32),
            ],
        ),
        out_shape=[
            jax.ShapeDtypeStruct((two, slots, rows, wide), BF),
            jax.ShapeDtypeStruct((two, 1, wide), F32),
        ],
        compiler_params=pltpu.CompilerParams(vmem_limit_bytes=56 * 2**20),
        cost_estimate=LITTLE,
        name="attend_back",
    )(me, qkv, context, d_context, log_total, cosine, sine)


def feed_kernel(count, first, *refs):
    pieces, w = refs[:count], refs[count]
    act, inner, slope, swish, held, in_sem, out_sem = refs[-7:]
    step = pl.program_id(0)
    height = pieces[0].shape[0]
    rows, ff = inner.shape
    each = rows // height

    def bring(i):
        return pltpu.make_async_copy(pieces[i], held.at[pl.ds(i * height, height)], in_sem.at[i])

    def put(i):
        return pltpu.make_async_copy(
            held.at[pl.ds(i * height, height)], act.at[pl.ds(first + i * height, height)], out_sem.at[i]
        )

    @pl.when(step == 0)
    def _():
        for i in range(count):
            bring(i).start()

    for k in range(count // each):

        @pl.when(step == k)
        def _(k=k):
            for i in range(k * each, (k + 1) * each):
                bring(i).wait()
                put(i).start()

    here = held[pl.ds(pl.multiple_of(step * rows, rows), rows), :]
    wide = dot(here, w[...])
    gate, upward = wide[:, :ff], wide[:, ff:]
    sigmoid = 1.0 / (1.0 + jnp.exp(-gate))
    product = gate * sigmoid
    inner[...] = (product * upward).astype(BF)
    swish[...] = product.astype(BF)
    slope[...] = (upward * sigmoid * (1.0 + gate * (1.0 - sigmoid))).astype(BF)

    @pl.when(step == count // each - 1)
    def _():
        for i in range(count):
            put(i).wait()


def feed(pieces, rows, w, earlier=None, total=None):
    count = len(pieces)
    height, width = pieces[0].shape
    ff = w.shape[1] // 2
    all_rows = count * height
    first = 0 if earlier is None else total - all_rows
    kept = () if earlier is None else earlier
    block = pl.BlockSpec((rows, ff), lambda i: (i + first // rows, 0))
    return pl.pallas_call(
        functools.partial(feed_kernel, count, first),
        grid=(all_rows // rows,),
        in_specs=[pl.BlockSpec(memory_space=pltpu.HBM)] * count
        + [pl.BlockSpec(w.shape, lambda i: (0, 0))]
        + [pl.BlockSpec(memory_space=pltpu.HBM)] * len(kept),
        out_specs=[pl.BlockSpec(memory_space=pltpu.HBM), block, block, block],
        out_shape=[jax.ShapeDtypeStruct((total, width), BF)] + [jax.ShapeDtypeStruct((total, ff), BF)] * 3,
        scratch_shapes=[
            pltpu.VMEM((all_rows, width), BF),
            pltpu.SemaphoreType.DMA((count,)),
            pltpu.SemaphoreType.DMA((count,)),
        ],
        input_output_aliases={count + 1 + i: i for i in range(len(kept))},
        compiler_params=pltpu.CompilerParams(vmem_limit_bytes=56 * 2**20),
        cost_estimate=pl.CostEstimate(
            flops=2 * all_rows * width * 2 * ff, bytes_accessed=2 * w.size, transcendentals=0
        ),
        name="feed",
    )(*pieces, w, *kept)


def feed_back_kernel(sends, *refs):
    cot, down, w, slope, swish = refs[:5]
    d_wide, sent, kept = refs[-3:]
    step = pl.program_id(0)
    d_inner = dot(cot[...], down[...])
    d_gate = (d_inner * slope[...].astype(F32)).astype(BF)
    d_upward = (d_inner * swish[...].astype(F32)).astype(BF)
    both = jnp.concatenate([d_gate, d_upward], 1)
    d_wide[...] = both
    result = dot_nt(both, w[...]).astype(BF)

    @pl.when(step < sends)
    def _():
        sent[0] = result

    @pl.when(step >= sends)
    def _():
        kept[0] = result


def feed_back(cot, down, w, slope, swish, slots, rows, earlier=None):
    total, width = cot.shape
    ff = down.shape[1]
    sends = len(slots) // 2
    first, stride = slots[0], 2

    def slot(i):
        return jnp.where(i < sends, first + stride * i, first - 1 + stride * (i - sends))

    def whole_of(v):
        return pl.BlockSpec(v.shape, lambda i: (0, 0))

    narrow = pl.BlockSpec((rows, ff), lambda i: (slot(i), 0))
    part = jax.ShapeDtypeStruct((sends, rows, width), BF)
    extra = () if earlier is None else (earlier,)
    return pl.pallas_call(
        functools.partial(feed_back_kernel, sends),
        grid=(2 * sends,),
        in_specs=[
            pl.BlockSpec((rows, width), lambda i: (slot(i), 0)),
            whole_of(down),
            whole_of(w),
            narrow,
            narrow,
        ]
        + [pl.BlockSpec(memory_space=pl.ANY)] * len(extra),
        out_specs=[
            pl.BlockSpec((rows, 2 * ff), lambda i: (slot(i), 0)),
            pl.BlockSpec((1, rows, width), lambda i: (jnp.minimum(i, sends - 1), 0, 0)),
            pl.BlockSpec((1, rows, width), lambda i: (jnp.maximum(i - sends, 0), 0, 0)),
        ],
        out_shape=[jax.ShapeDtypeStruct((total, 2 * ff), BF), part, part],
        input_output_aliases={5: 0} if extra else {},
        compiler_params=pltpu.CompilerParams(vmem_limit_bytes=56 * 2**20),
        cost_estimate=pl.CostEstimate(
            flops=2 * 2 * sends * rows * width * 3 * ff,
            bytes_accessed=2 * (w.size + down.size + 2 * sends * rows * (2 * width + 4 * ff)),
            transcendentals=0,
        ),
        name="feed_back",
    )(cot, down, w, slope, swish, *extra)


def over_rows_kernel(*refs):
    out, start = refs[-1], 0
    for left, right in zip(refs[:-1:2], refs[1:-1:2]):
        stop = start + right.shape[1]
        out[:, start:stop] = over_rows(left[...], right[...]).astype(BF)
        start = stop


def weight_grad(*pairs, tile=512):
    rows, width = pairs[0][0].shape
    cols = sum(right.shape[1] for _, right in pairs)
    specs = []
    for _, right in pairs:
        specs += [pl.BlockSpec((rows, tile), lambda i: (0, i)), pl.BlockSpec(right.shape, lambda i: (0, 0))]
    return pl.pallas_call(
        over_rows_kernel,
        grid=(width // tile,),
        in_specs=specs,
        out_specs=pl.BlockSpec((tile, cols), lambda i: (i, 0)),
        out_shape=jax.ShapeDtypeStruct((width, cols), BF),
        compiler_params=pltpu.CompilerParams(vmem_limit_bytes=56 * 2**20),
        cost_estimate=LITTLE,
        name="weight_grad",
    )(*(v for pair in pairs for v in pair))


def project_kernel(count, *refs):
    pieces, w = refs[:count], refs[count]
    all_rows, out, held, in_sem, out_sem = refs[-5:]
    step = pl.program_id(0)
    starts = [sum(p.shape[0] for p in pieces[:i]) for i in range(count)]
    rows = out.shape[0]

    def bring(i):
        return pltpu.make_async_copy(pieces[i], held.at[pl.ds(starts[i], pieces[i].shape[0])], in_sem.at[i])

    def put(i):
        at = pl.ds(starts[i], pieces[i].shape[0])
        return pltpu.make_async_copy(held.at[at], all_rows.at[at], out_sem.at[i])

    @pl.when(step == 0)
    def _():
        for i in range(count):
            bring(i).start()

    for k in range(held.shape[0] // rows):

        @pl.when(step == k)
        def _(k=k):
            for i in range(count):
                if k * rows <= starts[i] < (k + 1) * rows:
                    bring(i).wait()
                    put(i).start()

    here = held[pl.ds(pl.multiple_of(step * rows, rows), rows), :]
    out[...] = dot(here, w[...]).astype(out.dtype)

    @pl.when(step == held.shape[0] // rows - 1)
    def _():
        for i in range(count):
            put(i).wait()


def project(pieces, rows, w, kind):
    total, width = sum(p.shape[0] for p in pieces), pieces[0].shape[1]
    cols = w.shape[1]
    return pl.pallas_call(
        functools.partial(project_kernel, len(pieces)),
        grid=(total // rows,),
        in_specs=[pl.BlockSpec(memory_space=pltpu.HBM)] * len(pieces) + [pl.BlockSpec(w.shape, lambda i: (0, 0))],
        out_specs=[pl.BlockSpec(memory_space=pltpu.HBM), pl.BlockSpec((rows, cols), lambda i: (i, 0))],
        out_shape=[jax.ShapeDtypeStruct((total, width), BF), jax.ShapeDtypeStruct((total, cols), kind)],
        scratch_shapes=[
            pltpu.VMEM((total, width), BF),
            pltpu.SemaphoreType.DMA((len(pieces),)),
            pltpu.SemaphoreType.DMA((len(pieces),)),
        ],
        compiler_params=pltpu.CompilerParams(vmem_limit_bytes=56 * 2**20),
        cost_estimate=LITTLE,
        name="project",
    )(*pieces, w)


FAR, NEAR = (7, 6), (1, 3, 5, 0, 2, 4)


def assemble_kernel(count, *refs):
    pieces, out, held, in_sem, out_sem = refs[:count], refs[count], *refs[count + 1 :]
    ins, outs, start = [], [], 0
    for i, piece in enumerate(pieces):
        at = pl.ds(start, piece.shape[0])
        ins.append(pltpu.make_async_copy(piece, held.at[at], in_sem.at[i]))
        outs.append(pltpu.make_async_copy(held.at[at], out.at[at], out_sem.at[i]))
        start += piece.shape[0]
    for copy in ins:
        copy.start()
    for one, two in zip(ins, outs):
        one.wait()
        two.start()
    for copy in outs:
        copy.wait()


def assemble(*pieces):
    rows, width = sum(p.shape[0] for p in pieces), pieces[0].shape[1]
    return pl.pallas_call(
        functools.partial(assemble_kernel, len(pieces)),
        in_specs=[pl.BlockSpec(memory_space=pl.ANY)] * len(pieces),
        out_specs=pl.BlockSpec(memory_space=pltpu.HBM),
        out_shape=jax.ShapeDtypeStruct((rows, width), pieces[0].dtype),
        scratch_shapes=[
            pltpu.VMEM((rows, width), pieces[0].dtype),
            pltpu.SemaphoreType.DMA((len(pieces),)),
            pltpu.SemaphoreType.DMA((len(pieces),)),
        ],
        compiler_params=pltpu.CompilerParams(vmem_limit_bytes=56 * 2**20),
        cost_estimate=LITTLE,
        name="assemble",
    )(*pieces)


def norm_kernel(count, *refs):
    terms, (base, gain, shift) = refs[:count], refs[count : count + 3]
    total, unit, inverse, low = refs[-4:]
    v = base[...].astype(F32)
    for t in terms:
        v = v + t[...].astype(F32)
    centered = v - jnp.mean(v, -1, keepdims=True)
    scale = lax.rsqrt(jnp.mean(centered * centered, -1, keepdims=True) + EPS)
    normed = centered * scale
    total[...] = v
    unit[...] = normed
    inverse[...] = jnp.broadcast_to(scale, inverse.shape)
    low[...] = (normed * gain[...] + shift[...]).astype(BF)


def in_rows(rows, cols):
    return pl.BlockSpec((rows, cols), lambda i: (i, 0))


def fixed(*dims):
    return pl.BlockSpec(dims, lambda i: (0,) * len(dims))


def norm(base, terms, gain, shift, step=64):
    rows, width = base.shape
    return pl.pallas_call(
        functools.partial(norm_kernel, len(terms)),
        grid=(rows // step,),
        in_specs=[in_rows(step, width)] * (len(terms) + 1) + [fixed(1, width)] * 2,
        out_specs=[in_rows(step, width), in_rows(step, width), in_rows(step, 128), in_rows(step, width)],
        out_shape=[
            jax.ShapeDtypeStruct((rows, width), F32),
            jax.ShapeDtypeStruct((rows, width), F32),
            jax.ShapeDtypeStruct((rows, 128), F32),
            jax.ShapeDtypeStruct((rows, width), BF),
        ],
        compiler_params=pltpu.CompilerParams(vmem_limit_bytes=56 * 2**20),
        cost_estimate=LITTLE,
        name="norm",
    )(*terms, base, gain[None], shift[None])


def norm_back_kernel(count, *refs):
    terms, (base, unit, inverse, gain) = refs[:count], refs[count : count + 4]
    total, sums, low = refs[-3:]
    upstream = terms[0][...].astype(F32)
    for t in terms[1:]:
        upstream = upstream + t[...].astype(F32)
    normed = unit[...]
    scaled = upstream * gain[...]
    product = upstream * normed
    adjusted = (
        scaled
        - jnp.mean(scaled, -1, keepdims=True)
        - normed * jnp.mean(product * gain[...], -1, keepdims=True)
    )
    v = base[...].astype(F32) + inverse[:, :1] * adjusted
    total[...] = v
    low[...] = v.astype(BF)
    here = jnp.concatenate([jnp.sum(product, 0, keepdims=True), jnp.sum(upstream, 0, keepdims=True)], 0)

    @pl.when(pl.program_id(0) == 0)
    def _():
        sums[...] = here

    @pl.when(pl.program_id(0) > 0)
    def _():
        sums[...] += here


def norm_back(base, terms, unit, inverse, gain, step=64):
    rows, width = base.shape
    return pl.pallas_call(
        functools.partial(norm_back_kernel, len(terms)),
        grid=(rows // step,),
        in_specs=[in_rows(step, width)] * (len(terms) + 2) + [in_rows(step, 128), fixed(1, width)],
        out_specs=[in_rows(step, width), fixed(2, width), in_rows(step, width)],
        out_shape=[
            jax.ShapeDtypeStruct((rows, width), F32),
            jax.ShapeDtypeStruct((2, width), F32),
            jax.ShapeDtypeStruct((rows, width), BF),
        ],
        compiler_params=pltpu.CompilerParams(vmem_limit_bytes=56 * 2**20),
        cost_estimate=LITTLE,
        name="norm_back",
    )(*terms, base, unit, inverse, gain[None])


class Place:
    def __init__(self, n_dp, n_tensor):
        self.n_dp, self.n_tensor = n_dp, n_tensor
        self.n_line = n_dp // 2
        dp, tensor = lax.axis_index("dp"), lax.axis_index("tensor")
        self.dp, self.tensor = dp, tensor
        self.line, self.pair = dp // 2, dp % 2

    def to_pair(self, v):
        return lax.ppermute(v, "dp", [(i, i ^ 1) for i in range(self.n_dp)])

    def to_side(self, v):
        return lax.ppermute(v, "tensor", [(i, i ^ 2) for i in range(self.n_tensor)])

    def to_core(self, v):
        return lax.ppermute(v, "tensor", [(i, i ^ 1) for i in range(self.n_tensor)])

    def by_pair(self, first, second, axis):
        return jnp.where(
            self.pair == 0,
            jnp.concatenate([first, second], axis),
            jnp.concatenate([second, first], axis),
        )

    def halves(self, v, axis):
        half = v.shape[axis] // 2
        low = lax.slice_in_dim(v, 0, half, axis=axis)
        high = lax.slice_in_dim(v, half, 2 * half, axis=axis)
        return jnp.where(self.pair == 0, low, high), jnp.where(self.pair == 0, high, low)

    def line_groups(self):
        return [[2 * i + p for i in range(self.n_line)] for p in (0, 1)]

    def widen(self, *weights):
        mine, theirs = zip(*[self.halves(w, 1) for w in weights])
        mine, theirs = jnp.concatenate(mine, 1), jnp.concatenate(theirs, 1)
        return mine, self.to_pair(theirs), theirs

    def gather_weight(self, mine, other):
        return self.gather_piece(self.by_pair(mine, other, 0))

    def gather_piece(self, piece):
        return lax.all_gather(piece, "dp", axis=0, tiled=True, axis_index_groups=self.line_groups())

    def scatter_grad(self, grad):
        return lax.psum_scatter(
            grad,
            "dp",
            scatter_dimension=0,
            tiled=True,
            axis_index_groups=self.line_groups(),
        )

    def share_send(self, total):
        mine, theirs = self.halves(total, 0)
        return mine, self.to_pair(theirs)

    def share_grad(self, mine, other, parts):
        cols = mine.shape[1] // parts
        shares = []
        for i in range(parts):
            at = slice(i * cols, (i + 1) * cols)
            shares.append(self.by_pair(mine[:, at], other[:, at], 1).astype(F32))
        return shares

    def gather_links(self, own):
        return own, self.to_side(own), self.to_pair(own)

    def gather_cores(self, own, side, pair):
        return own, self.to_core(own), side, self.to_core(side), pair, self.to_core(pair)

    def gather_begin(self, own):
        return self.gather_cores(*self.gather_links(own))

    def gather_end(self, near):
        side, pair = near[2], near[4]
        half = side.shape[0] // 2
        one, two = lax.optimization_barrier((side[:half], pair[half:]))
        d1, d2 = self.to_pair(one), self.to_side(two)
        return (d1, d2, self.to_core(d1), self.to_core(d2)), one, two

    def core_sum(self, far, far_sent):
        half = far.shape[0] // 2
        other = self.to_core(far_sent)
        return tuple(
            (far[i].astype(F32) + other[i].astype(F32)).astype(BF)
            for i in (slice(0, half), slice(half, 2 * half))
        )

    def core_sums(self, near, near_sent):
        other = self.to_core(near_sent)
        own, side, pair = (near[k].astype(F32) + other[k].astype(F32) for k in range(3))
        return side, pair, own

    def scatter_begin(self, far, far_sent, near, near_sent):
        return (*self.core_sum(far, far_sent), *self.core_sums(near, near_sent))

    def scatter_begin_once(self, far, far_sent, near, near_sent):
        half = far.shape[0] // 2
        other = self.to_core(jnp.concatenate([far_sent[None], near_sent], 0))
        f1, f2 = (
            (far[i].astype(F32) + other[0, i].astype(F32)).astype(BF)
            for i in (slice(0, half), slice(half, 2 * half))
        )
        own, side, pair = (near[k].astype(F32) + other[k + 1].astype(F32) for k in range(3))
        return f1, f2, side, pair, own

    def scatter_far(self, f1, f2):
        return self.to_pair(f1), self.to_side(f2)

    def scatter_add(self, d1, d2, side, pair, own):
        none = jnp.zeros_like(d1)
        side = (side + jnp.concatenate([d1, none], 0).astype(F32)).astype(BF)
        pair = (pair + jnp.concatenate([none, d2], 0).astype(F32)).astype(BF)
        return side, pair, own

    def scatter_middle(self, begun, *hold):
        f1, f2, side, pair, own = begun
        d1, d2 = self.scatter_far(f1, f2)
        if hold:
            d1, d2, side, pair = all_after((d1, d2, side, pair), *hold)
        return self.scatter_add(d1, d2, side, pair, own)

    def scatter_end(self, middle):
        side, pair, own = middle
        return own, self.to_side(side), self.to_pair(pair)

    def scatter_rows(self, *parts):
        return self.scatter_end(self.scatter_middle(self.scatter_begin(*parts)))

    def sum_all(self, v):
        for axis, size in (("tensor", self.n_tensor), ("dp", self.n_dp)):
            step = 1
            while step < size:
                others = [
                    lax.ppermute(v, axis, [(i, i ^ (k * step)) for i in range(size)])
                    for k in range(1, 4 if 4 * step <= size else 2)
                ]
                v = v + others[0]
                if len(others) == 3:
                    v = v + (others[1] + others[2])
                step *= 1 + len(others)
        return v


def local(
    n_dp,
    n_tensor,
    block_input,
    cotangent,
    ln1_gain,
    ln1_bias,
    w_query,
    q_bias,
    w_key,
    k_bias,
    w_value,
    v_bias,
    w_out,
    ln2_gain,
    ln2_bias,
    w_gate,
    w_up,
    w_down,
):
    at = Place(n_dp, n_tensor)
    width = block_input.shape[1]
    rows = block_input.shape[0]
    length = rows * n_tensor
    half = rows // 2
    cols = w_query.shape[1] // 2
    heads = cols // HEAD
    ff = w_gate.shape[1] // 2

    def in_halves(v):
        return v[:half], v[half:]

    first_mine, first_other, first_sent = at.widen(w_query, w_key, w_value, w_out)
    _, unit_one, inverse_one, act = norm(after(block_input, first_sent), (), ln1_gain, ln1_bias)
    first_piece = at.by_pair(*all_after((first_mine, first_other), act), 0)
    full_qkv = at.gather_piece(first_piece[:, : 3 * cols])
    full_out = at.gather_piece(first_piece[:, 3 * cols :])
    near = at.gather_begin(act)
    far, *halves = at.gather_end(near)
    rest_mine, rest_other, _ = at.widen(*all_after((w_gate, w_up, w_down), *halves))
    tokens = 8 * rows
    cut = 6 * rows

    slots = after(jnp.arange(n_tensor), act)
    place = ((at.tensor ^ slots)[:, None] * rows + jnp.arange(rows)[None, :]).reshape(length)
    cosine, sine = (v.reshape(n_tensor, rows, 128) for v in turn_tables(place))
    me = at.tensor.astype(jnp.int32).reshape(1)

    column = at.tensor * 2 * cols + at.pair * cols
    query_shift = lax.dynamic_slice_in_dim(q_bias, column, cols)
    value_shift = lax.dynamic_slice_in_dim(v_bias, column, cols)
    key_column = at.tensor * 2 * heads * ROT + at.pair * heads * ROT
    key_rows = lax.dynamic_slice_in_dim(k_bias, key_column, heads * ROT)
    key_shift = jnp.pad(key_rows.reshape(heads, ROT), ((0, 0), (0, HEAD - ROT))).reshape(cols)
    shift = jnp.concatenate([query_shift, key_shift, value_shift])[None]

    far = all_after(far, cosine, sine, shift)
    act_one, pre = project([*near, *far], rows, full_qkv, F32)
    pre = pre.reshape(2, n_tensor, rows, 3 * cols)
    rest_late = after(rest_other, pre)
    wide_piece = at.by_pair(rest_mine[:, : 2 * ff], rest_late[:, : 2 * ff], 0)
    down_piece = at.by_pair(rest_mine[:, 2 * ff :], rest_late[:, 2 * ff :], 0)
    full_wide = at.gather_piece(wide_piece)
    qkv, context, log_total = attend(me, after(pre, wide_piece, down_piece), shift, cosine, sine)
    context_all = context.reshape(tokens, cols)

    def product(left, right):
        far = times_transposed(left[cut:], right).astype(BF)
        far, far_sent = lax.optimization_barrier((far[:rows], far[rows:]))
        near = times_transposed(after(left[:cut], far_sent), right).astype(BF)
        near = near.reshape(3, 2, rows, width)
        return far, far_sent, near[:, 0], near[:, 1]

    mixed = at.scatter_rows(*product(context_all, full_out))
    hidden, unit_two, inverse_two, act = norm(block_input, mixed, ln2_gain, ln2_bias)
    full_down = at.gather_piece(after(down_piece, act))
    near = at.gather_begin(act)
    far, *_ = at.gather_end(near)
    fed_near = feed(near, rows, full_wide, total=tokens)
    cot_links = at.gather_links(after(cotangent, *far))
    act_two, inner, slope, swish = feed(far, rows, full_wide, fed_near, tokens)
    cot_near = at.gather_cores(*all_after(cot_links, fed_near[1]))
    cot_far, *_ = at.gather_end(cot_near)
    cot_all = assemble(*all_after((*cot_near, *cot_far), inner))
    down_grad = weight_grad((cot_all, inner))
    down_total = at.scatter_grad(down_grad)
    d_wide, far_sent, far_kept = feed_back(
        after(cot_all, down_grad), full_down, full_wide, slope, swish, FAR, rows
    )
    far_sum = at.core_sum(far_kept[0], far_sent[0])
    d_wide, near_sent, near_kept = feed_back(
        after(cot_all, *far_sum), full_down, full_wide, slope, swish, NEAR, rows, d_wide
    )
    d1, d2, near_kept, near_sent, d_wide = lax.optimization_barrier(
        (*at.scatter_far(*far_sum), near_kept, near_sent, d_wide)
    )
    middle = at.scatter_add(d1, d2, *at.core_sums(near_kept, near_sent))
    wide_grad = weight_grad((act_two, after(d_wide, *middle)))
    d_act_two = at.scatter_end(middle)
    *d_act_two, wide_grad, down_total = lax.optimization_barrier((*d_act_two, wide_grad, down_total))
    wide_total = at.scatter_grad(wide_grad)
    d_hidden, sums_two, low = norm_back(
        cotangent, d_act_two, unit_two, inverse_two, ln2_gain
    )
    links = at.gather_links(low)
    fed_parts = product(after(inner, low), full_down)
    own, side, pair, *fed_parts = lax.optimization_barrier((*links, *fed_parts))
    near = at.gather_cores(own, side, pair)
    far, *_ = at.gather_end(near)
    fed_begun = at.scatter_begin_once(*fed_parts)
    *far, f1, f2 = lax.optimization_barrier((*far, *fed_begun[:2]))
    fed_begun = (f1, f2, *fed_begun[2:])
    d_hidden_all, d_context = project([*near, *far], rows, full_out, BF)
    d_context = d_context.reshape(context.shape)
    fed_middle = at.scatter_middle(fed_begun, d_context)
    down_sent = at.share_send(after(down_total, d_hidden_all))
    fed = at.scatter_end(fed_middle)
    d_qkv, sums = attend_back(me, qkv, context, after(d_context, *fed_middle), log_total, cosine, sine)
    d_qkv, *fed = lax.optimization_barrier((d_qkv, *fed, *down_sent))
    *fed, down_mine, down_other = fed
    d_qkv = d_qkv.reshape(tokens, 3 * cols)
    sums = sums[0, 0] + sums[1, 0]
    qkvo_grad = weight_grad((act_one, d_qkv), (d_hidden_all, context_all))
    qkvo_total = at.scatter_grad(qkvo_grad)
    d_qkv, wide_total = all_after((d_qkv, wide_total), qkvo_grad)
    begun = at.scatter_begin(*product(d_qkv, full_qkv))
    *begun, wide_mine, wide_other = lax.optimization_barrier((*begun, *at.share_send(wide_total)))
    middle = at.scatter_middle(begun)
    block_output = (hidden + fed[0] + fed[1].astype(F32) + fed[2].astype(F32)).astype(BF)
    d_act_one = at.scatter_end(middle)
    (down_share,) = at.share_grad(*all_after((down_mine, down_other), *middle), 1)
    gate_share, up_share = at.share_grad(*all_after((wide_mine, wide_other), *middle), 2)
    input_grad, sums_one, _ = norm_back(d_hidden, d_act_one, unit_one, inverse_one, ln1_gain)
    query_share, key_share, value_share, out_share = at.share_grad(
        *at.share_send(after(qkvo_total, sums_one)), 4
    )

    query_part, value_part = sums[:cols], sums[2 * cols :]
    key_part = sums[cols : 2 * cols].reshape(heads, HEAD)[:, :ROT].reshape(heads * ROT)
    query_full = lax.dynamic_update_slice(jnp.zeros(q_bias.shape, F32), query_part, (column,))
    value_full = lax.dynamic_update_slice(jnp.zeros(v_bias.shape, F32), value_part, (column,))
    key_full = lax.dynamic_update_slice(jnp.zeros(k_bias.shape, F32), key_part, (key_column,))
    sums = at.sum_all(
        jnp.concatenate([sums_one[0], sums_one[1], sums_two[0], sums_two[1], query_full, value_full, key_full])
    )
    n = width
    return (
        block_output,
        input_grad,
        sums[:n],
        sums[n : 2 * n],
        query_share,
        sums[4 * n : 5 * n],
        key_share,
        sums[6 * n :],
        value_share,
        sums[5 * n : 6 * n],
        out_share,
        sums[2 * n : 3 * n],
        sums[3 * n : 4 * n],
        gate_share,
        up_share,
        down_share,
    )


def solution(mesh):
    rows = P(("dp", "tensor"), None)
    matrix = P("dp", "tensor")
    return jax.shard_map(
        functools.partial(local, mesh.shape["dp"], mesh.shape["tensor"]),
        mesh=mesh,
        in_specs=(
            rows, rows, P(), P(), matrix, P(), matrix, P(), matrix, P(), matrix, P(), P(),
            matrix, matrix, matrix,
        ),
        out_specs=(
            rows, rows, P(), P(), matrix, P(), matrix, P(), matrix, P(), matrix, P(), P(),
            matrix, matrix, matrix,
        ),
        check_vma=False,
    )
```

profile of v0, /device:TPU:0, one launch (start us, length us, event | category | flops | bytes accessed | tf_op | source)
XLA Modules:
  0.0 611.6 jit_solution(2615967364729787092)
XLA Ops:
  18.7 7.6 %collective-permute-done.9 = bf16[256,1024]{1,0:T(8,128)(2,1)S(1)} collective-permute-done((bf16[256,1024]{1,0:T(8,128)(2,1)S(1)}, bf16[256,1024]{1,0:T(8,128)(2,1)S(1)}, u32[]{:S(2)}, u32[]{:S(2)}) %collective-permute-start.9) | collective-permute-done | bytes 524320 | tf_op jit(solution)/shard_map/ppermute | solution.py:593
  34.3 18.2 %collective-permute-done.3.refs_4_ = bf16[256,2048]{1,0:T(8,128)(2,1)} collective-permute-done((bf16[256,2048]{1,0:T(8,128)(2,1)}, bf16[256,2048]{1,0:T(8,128)(2,1)}, u32[]{:S(2)}, u32[]{:S(2)}) %collective-permute-start.3) | collective-permute-done | bytes 1048608 | tf_op jit(solution)/shard_map/ppermute | solution.py:593
  64.2 7.1 %collective-permute-done.5.refs_6_ = bf16[128,2048]{1,0:T(8,128)(2,1)S(1)} collective-permute-done((bf16[128,2048]{1,0:T(8,128)(2,1)}, bf16[128,2048]{1,0:T(8,128)(2,1)S(1)}, u32[]{:S(2)}, u32[]{:S(2)}) %collective-permute-start.5) | collective-permute-done | bytes 524320 | tf_op jit(solution)/shard_map/ppermute | solution.py:593
  79.3 13.5 %all-gather.5.cloned.1.call-done.refs_10_ = bf16[2048,768]{1,0:T(8,128)(2,1)} async-done(((bf16[512,768]{1,0:T(8,128)(2,1)}), bf16[2048,768]{1,0:T(8,128)(2,1)}) %all-gather.5.cloned.1.call-update) | async-done | bytes 3145744 | tf_op jit(solution)/shard_map/all_gather | solution.py:626
  92.8 12.8 %project.2 = (bf16[2048,2048]{1,0:T(8,128)(2,1)}, f32[2048,768]{1,0:T(8,128)}) custom-call(bf16[256,2048]{1,0:T(8,128)(2,1)} %get-tuple-element.150.refs_0_, bf16[256,2048]{1,0:T(8,128)(2,1)} %collective-permute-done.refs_1_, bf16[256,2048]{1,0:T(8,128)(2,1)} %collective-permute-done.1.refs_2_, bf16[256,2048]{1,0:T(8,128)(2,1)} %collective-permute-done.2.refs_3_, ...), custom_call_target="tpu_custom_call" | custom-call | tf_op jit(solution)/shard_map/project/pallas_call | solution.py:441
  113.2 12.4 %attend.1 = (bf16[2,4,256,768]{3,2,1,0:T(8,128)(2,1)S(1)}, bf16[2,4,256,256]{3,2,1,0:T(8,128)(2,1)S(1)}, f32[2,4,8,256]{3,2,1,0:T(8,128)S(1)}) custom-call(s32[1]{0:T(128)} %bitcast.me, f32[2,4,256,768]{3,2,1,0:T(8,128)S(1)} %bitcast.136, f32[1,768]{1,0:T(1,128)S(1)} %broadcast_in_dim.33.shift, f32[4,256,128]{2,1,0:T(8,128)S(1)} %concatenate.118.cosine, ...), custom_call_target="tpu_custom_call" | custom-call | tf_op jit(solution)/shard_map/attend/pallas_call | solution.py:117
  144.2 11.0 %collective-permute-done.15 = bf16[128,2048]{1,0:T(8,128)(2,1)S(1)} collective-permute-done((bf16[128,2048]{1,0:T(8,128)(2,1)S(1)}, bf16[128,2048]{1,0:T(8,128)(2,1)S(1)}, u32[]{:S(2)}, u32[]{:S(2)}) %collective-permute-start.15) | collective-permute-done | bytes 524320 | tf_op jit(solution)/shard_map/ppermute | solution.py:596
  161.5 22.1 %collective-permute-done.16.refs_2_ = bf16[256,2048]{1,0:T(8,128)(2,1)S(1)} collective-permute-done((bf16[256,2048]{1,0:T(8,128)(2,1)S(1)}, bf16[256,2048]{1,0:T(8,128)(2,1)S(1)}, u32[]{:S(2)}, u32[]{:S(2)}) %collective-permute-start.16) | collective-permute-done | bytes 1048608 | tf_op jit(solution)/shard_map/ppermute | solution.py:593
  193.0 22.0 %collective-permute-done.18.refs_4_ = bf16[256,2048]{1,0:T(8,128)(2,1)S(1)} collective-permute-done((bf16[256,2048]{1,0:T(8,128)(2,1)}, bf16[256,2048]{1,0:T(8,128)(2,1)S(1)}, u32[]{:S(2)}, u32[]{:S(2)}) %collective-permute-start.18) | collective-permute-done | bytes 1048608 | tf_op jit(solution)/shard_map/ppermute | solution.py:593
  218.1 8.7 %collective-permute-done.19.refs_0_ = bf16[128,2048]{1,0:T(8,128)(2,1)S(1)} collective-permute-done((bf16[128,2048]{1,0:T(8,128)(2,1)S(1)}, bf16[128,2048]{1,0:T(8,128)(2,1)S(1)}, u32[]{:S(2)}, u32[]{:S(2)}) %collective-permute-start.19) | collective-permute-done | bytes 524320 | tf_op jit(solution)/shard_map/ppermute | solution.py:593
  233.2 17.9 %feed.2 = (bf16[2048,2048]{1,0:T(8,128)(2,1)}, bf16[2048,704]{1,0:T(8,128)(2,1)}, bf16[2048,704]{1,0:T(8,128)(2,1)}, bf16[2048,704]{1,0:T(8,128)(2,1)}) custom-call(bf16[256,2048]{1,0:T(8,128)(2,1)} %get-tuple-element.172.refs_0_, bf16[256,2048]{1,0:T(8,128)(2,1)} %copy-done.58, bf16[256,2048]{1,0:T(8,128)(2,1)} %copy-done.55, ...), custom_call_target="tpu_custom_call" | custom-call | flops 8858370048 | bytes 5767168 | tf_op jit(solution)/shard_map/feed/pallas_call | solution.py:290
  257.8 10.6 %collective-permute-done.31.refs_6_ = bf16[128,2048]{1,0:T(8,128)(2,1)S(1)} collective-permute-done((bf16[128,2048]{1,0:T(8,128)(2,1)S(1)}, bf16[128,2048]{1,0:T(8,128)(2,1)S(1)}, u32[]{:S(2)}, u32[]{:S(2)}) %collective-permute-start.31) | collective-permute-done | bytes 524320 | tf_op jit(solution)/shard_map/ppermute | solution.py:593
  269.2 9.4 %feed.3 = (bf16[2048,2048]{1,0:T(8,128)(2,1)}, bf16[2048,704]{1,0:T(8,128)(2,1)}, bf16[2048,704]{1,0:T(8,128)(2,1)}, bf16[2048,704]{1,0:T(8,128)(2,1)}) custom-call(bf16[128,2048]{1,0:T(8,128)(2,1)} %copy-done.39, bf16[128,2048]{1,0:T(8,128)(2,1)} %copy-done.40, ...), custom_call_target="tpu_custom_call", output_to_operand_aliasing={{0}: (5, {}), {1}: (6, {}), {2}: (7, {}), {3}: (8, {})} | custom-call | flops 2952790016 | bytes 5767168 | tf_op jit(solution)/shard_map/feed/pallas_call | solution.py:290
  286.8 10.9 %weight_grad.3 = bf16[2048,704]{1,0:T(8,128)(2,1)} custom-call(bf16[2048,2048]{1,0:T(8,128)(2,1)} %assemble.1.refs_0_, bf16[2048,704]{1,0:T(8,128)(2,1)} %get-tuple-element.220.refs_1_), custom_call_target="tpu_custom_call" | custom-call | tf_op jit(solution)/shard_map/weight_grad/pallas_call | solution.py:389
  297.7 12.7 %feed_back.2 = (bf16[2048,1408]{1,0:T(8,128)(2,1)}, bf16[1,256,2048]{2,1,0:T(8,128)(2,1)}, bf16[1,256,2048]{2,1,0:T(8,128)(2,1)}) custom-call(bf16[2048,2048]{1,0:T(8,128)(2,1)} %assemble.1.refs_0_, bf16[2048,704]{1,0:T(8,128)(2,1)} %all-gather.11.cloned.1.call-done.refs_1_, bf16[2048,1408]{1,0:T(8,128)(2,1)} %all-gather.9.cloned.1.call-done.refs_6_.refs_4_.refs_2_, ...), custom_call_target="tpu_custom_call" | custom-call | flops 4429185024 | bytes 15728640 | tf_op jit(solution)/shard_map/feed_back/pallas_call | solution.py:347
  315.5 26.8 %feed_back.3 = (bf16[2048,1408]{1,0:T(8,128)(2,1)}, bf16[3,256,2048]{2,1,0:T(8,128)(2,1)}, bf16[3,256,2048]{2,1,0:T(8,128)(2,1)}) custom-call(bf16[2048,2048]{1,0:T(8,128)(2,1)} %assemble.1.refs_0_, bf16[2048,704]{1,0:T(8,128)(2,1)} %all-gather.11.cloned.1.call-done.refs_1_, ...), custom_call_target="tpu_custom_call", output_to_operand_aliasing={{0}: (5, {})} | custom-call | flops 13287555072 | bytes 29884416 | tf_op jit(solution)/shard_map/feed_back/pallas_call | solution.py:347
  356.1 18.2 %weight_grad.4 = bf16[2048,1408]{1,0:T(8,128)(2,1)} custom-call(bf16[2048,2048]{1,0:T(8,128)(2,1)} %get-tuple-element.211.refs_0_, bf16[2048,1408]{1,0:T(8,128)(2,1)} %get-tuple-element.213.refs_1_), custom_call_target="tpu_custom_call" | custom-call | tf_op jit(solution)/shard_map/weight_grad/pallas_call | solution.py:389
  394.2 13.9 %collective-permute-done.42.refs_4_ = bf16[256,2048]{1,0:T(8,128)(2,1)S(1)} collective-permute-done((bf16[256,2048]{1,0:T(8,128)(2,1)}, bf16[256,2048]{1,0:T(8,128)(2,1)S(1)}, u32[]{:S(2)}, u32[]{:S(2)}) %collective-permute-start.42) | collective-permute-done | bytes 1048608 | tf_op jit(solution)/shard_map/ppermute | solution.py:593
  412.4 11.5 %collective-permute-done.46.refs_6_ = bf16[128,2048]{1,0:T(8,128)(2,1)S(1)} collective-permute-done((bf16[128,2048]{1,0:T(8,128)(2,1)S(1)}, bf16[128,2048]{1,0:T(8,128)(2,1)S(1)}, u32[]{:S(2)}, u32[]{:S(2)}) %collective-permute-start.46) | collective-permute-done | bytes 524320 | tf_op jit(solution)/shard_map/ppermute | solution.py:593
  432.3 8.7 %project.3 = (bf16[2048,2048]{1,0:T(8,128)(2,1)}, bf16[2048,256]{1,0:T(8,128)(2,1)}) custom-call(bf16[256,2048]{1,0:T(8,128)(2,1)} %get-tuple-element.224.refs_0_, bf16[256,2048]{1,0:T(8,128)(2,1)} %copy-done.25, bf16[256,2048]{1,0:T(8,128)(2,1)} %copy-done.15, bf16[256,2048]{1,0:T(8,128)(2,1)} %copy-done.24, bf16[256,2048]{1,0:T(8,128)(2,1)} %copy-done.14, ...), custom_call_target="tpu_custom_call" | custom-call | tf_op jit(solution)/shard_map/project/pallas_call | solution.py:441
  449.2 27.8 %attend_back.1 = (bf16[2,4,256,768]{3,2,1,0:T(8,128)(2,1)}, f32[2,1,768]{2,1,0:T(1,128)}) custom-call(s32[1]{0:T(128)} %bitcast.me, bf16[2,4,256,768]{3,2,1,0:T(8,128)(2,1)} %copy-done.4, bf16[2,4,256,256]{3,2,1,0:T(8,128)(2,1)} %copy-done, bf16[2,4,256,256]{3,2,1,0:T(8,128)(2,1)} %bitcast.146, f32[2,4,8,256]{3,2,1,0:T(8,128)} %copy-done.5, ...), custom_call_target="tpu_custom_call" | custom-call | tf_op jit(solution)/shard_map/attend_back/pallas_call | solution.py:207
  479.5 15.4 %weight_grad.5 = bf16[2048,1024]{1,0:T(8,128)(2,1)} custom-call(bf16[2048,2048]{1,0:T(8,128)(2,1)} %get-tuple-element.255.refs_0_, bf16[2048,768]{1,0:T(8,128)(2,1)} %bitcast.139, bf16[2048,2048]{1,0:T(8,128)(2,1)} %get-tuple-element.248.refs_2_, bf16[2048,256]{1,0:T(8,128)(2,1)} %bitcast.135), custom_call_target="tpu_custom_call" | custom-call | tf_op jit(solution)/shard_map/weight_grad/pallas_call | solution.py:389
  531.8 10.5 %collective-permute-done.61 = bf16[128,2048]{1,0:T(8,128)(2,1)} collective-permute-done((bf16[128,2048]{1,0:T(8,128)(2,1)}, bf16[128,2048]{1,0:T(8,128)(2,1)}, u32[]{:S(2)}, u32[]{:S(2)}) %collective-permute-start.61) | collective-permute-done | bytes 524320 | tf_op jit(solution)/shard_map/ppermute | solution.py:596
  552.2 15.7 %collective-permute-done.62.refs_2_ = bf16[256,2048]{1,0:T(8,128)(2,1)S(1)} collective-permute-done((bf16[256,2048]{1,0:T(8,128)(2,1)S(1)}, bf16[256,2048]{1,0:T(8,128)(2,1)S(1)}, u32[]{:S(2)}, u32[]{:S(2)}) %collective-permute-start.62) | collective-permute-done | bytes 1048608 | tf_op jit(solution)/shard_map/ppermute | solution.py:593
  (386 shorter events, 250.5 us)
Async XLA Ops:
  7.2 85.7 %all-gather.5.cloned.1.call-start = ((), (), s32[]{:S(2)}) async-start(), calls=%async_computation.3 | async-start | bytes 3932160 | tf_op jit(solution)/shard_map/all_gather | solution.py:626
  27.7 100.2 %all-gather.7.cloned.1.call-start = ((), (), s32[]{:S(2)}) async-start(), calls=%async_computation.4 | async-start | bytes 1310720 | tf_op jit(solution)/shard_map/all_gather | solution.py:626
  27.8 24.7 %collective-permute-start.3 = (bf16[256,2048]{1,0:T(8,128)(2,1)}, bf16[256,2048]{1,0:T(8,128)(2,1)}, u32[]{:S(2)}, u32[]{:S(2)}) collective-permute-start(bf16[256,2048]{1,0:T(8,128)(2,1)} %get-tuple-element.150.refs_0_), channel_id=1, source_target_pairs={{0,4},{4,0},{8,12},{12,8},{16,20},{20,16},{24,28},{28,24},{1,5},{5... | collective-permute-start | bytes 3145736 | tf_op jit(solution)/shard_map/ppermute | solution.py:593
  29.6 24.8 %collective-permute-start.1 = (bf16[256,2048]{1,0:T(8,128)(2,1)}, bf16[256,2048]{1,0:T(8,128)(2,1)}, u32[]{:S(2)}, u32[]{:S(2)}) collective-permute-start(bf16[256,2048]{1,0:T(8,128)(2,1)} %get-tuple-element.150.refs_0_), channel_id=1, source_target_pairs={{0,2},{1,3},{2,0},{3,1},{4,6},{5,7},{6,4},{7,5},{8,10},{9,11},{10,... | collective-permute-start | bytes 3145736 | tf_op jit(solution)/shard_map/ppermute | solution.py:596
  31.1 48.2 %collective-permute-start = (bf16[256,2048]{1,0:T(8,128)(2,1)}, bf16[256,2048]{1,0:T(8,128)(2,1)}, u32[]{:S(2)}, u32[]{:S(2)}) collective-permute-start(bf16[256,2048]{1,0:T(8,128)(2,1)} %get-tuple-element.150.refs_0_), channel_id=1, source_target_pairs={{0,1},{1,0},{2,3},{3,2},{4,5},{5,4},{6,7},{7,6},{8,9},{9,8},{10,11... | collective-permute-start | bytes 3145736 | tf_op jit(solution)/shard_map/ppermute | solution.py:599
  34.3 198.9 %all-gather.9.cloned.1.call-start = ((), (), s32[]{:S(2)}) async-start(), calls=%async_computation.5 | async-start | bytes 7208960 | tf_op jit(solution)/shard_map/all_gather | solution.py:626
  63.7 41.9 %collective-permute-start.10 = (bf16[256,2112]{0,1:T(8,128)(2,1)}, bf16[256,2112]{0,1:T(8,128)(2,1)}, u32[]{:S(2)}, u32[]{:S(2)}) collective-permute-start(bf16[256,2112]{0,1:T(8,128)(2,1)} %copy.45), channel_id=1, source_target_pairs={{0,4},{4,0},{8,12},{12,8},{16,20},{20,16},{24,28},{28,24},{1,5},{5... | collective-permute-start | bytes 3244040 | tf_op jit(solution)/shard_map/ppermute | solution.py:593
  109.1 188.6 %all-gather.11.cloned.1.call-start = ((), (), s32[]{:S(2)}) async-start(), calls=%async_computation.6 | async-start | bytes 3932160 | tf_op jit(solution)/shard_map/all_gather | solution.py:626
  159.5 24.2 %collective-permute-start.16 = (bf16[256,2048]{1,0:T(8,128)(2,1)S(1)}, bf16[256,2048]{1,0:T(8,128)(2,1)S(1)}, u32[]{:S(2)}, u32[]{:S(2)}) collective-permute-start(bf16[256,2048]{1,0:T(8,128)(2,1)S(1)} %get-tuple-element.287), channel_id=1, source_target_pairs={{0,4},{4,0},{8,12},{12,8},{16,20},{20,16},{24,28},{28,24},{1,5},{5... | collective-permute-start | bytes 3145736 | tf_op jit(solution)/shard_map/ppermute | solution.py:593
  161.0 23.9 %collective-permute-start.14 = (bf16[256,2048]{1,0:T(8,128)(2,1)S(1)}, bf16[256,2048]{1,0:T(8,128)(2,1)S(1)}, u32[]{:S(2)}, u32[]{:S(2)}) collective-permute-start(bf16[256,2048]{1,0:T(8,128)(2,1)S(1)} %get-tuple-element.288), channel_id=1, source_target_pairs={{0,2},{1,3},{2,0},{3,1},{4,6},{5,7},{6,4},{7,5},{8,10},{9,11},{10,... | collective-permute-start | bytes 3145736 | tf_op jit(solution)/shard_map/ppermute | solution.py:596
  191.4 182.9 %reduce-scatter.4.cloned.1.call-start = ((), (), s32[]{:S(2)}) async-start(), calls=%async_computation.7 | async-start | bytes 3932160 | tf_op jit(solution)/shard_map/reduce_scatter | solution.py:629
  229.5 25.2 %collective-permute-start.24 = (bf16[256,2048]{1,0:T(8,128)(2,1)S(1)}, bf16[256,2048]{1,0:T(8,128)(2,1)S(1)}, u32[]{:S(2)}, u32[]{:S(2)}) collective-permute-start(bf16[256,2048]{1,0:T(8,128)(2,1)S(1)} %copy-done.11), channel_id=1, source_target_pairs={{0,4},{4,0},{8,12},{12,8},{16,20},{20,16},{24,28},{28,24},{1,5},{5... | collective-permute-start | bytes 3145736 | tf_op jit(solution)/shard_map/ppermute | solution.py:593
  230.5 24.9 %collective-permute-start.23 = (bf16[256,2048]{1,0:T(8,128)(2,1)S(1)}, bf16[256,2048]{1,0:T(8,128)(2,1)S(1)}, u32[]{:S(2)}, u32[]{:S(2)}) collective-permute-start(bf16[256,2048]{1,0:T(8,128)(2,1)S(1)} %copy-done.11), channel_id=1, source_target_pairs={{0,2},{1,3},{2,0},{3,1},{4,6},{5,7},{6,4},{7,5},{8,10},{9,11},{10,... | collective-permute-start | bytes 3145736 | tf_op jit(solution)/shard_map/ppermute | solution.py:596
  310.7 184.2 %reduce-scatter.6.cloned.1.call-start = ((), (), s32[]{:S(2)}) async-start(), calls=%async_computation.8 | async-start | bytes 7208960 | tf_op jit(solution)/shard_map/reduce_scatter | solution.py:629
  313.7 28.6 %collective-permute-start.37 = (bf16[128,2048]{1,0:T(8,128)(2,1)S(1)}, bf16[128,2048]{1,0:T(8,128)(2,1)S(1)}, u32[]{:S(2)}, u32[]{:S(2)}) collective-permute-start(bf16[128,2048]{1,0:T(8,128)(2,1)S(1)} %get-tuple-element.305), channel_id=1, source_target_pairs={{0,2},{1,3},{2,0},{3,1},{4,6},{5,7},{6,4},{7,5},{8,10},{9,11},{10,... | collective-permute-start | bytes 1572872 | tf_op jit(solution)/shard_map/ppermute | solution.py:596
  314.5 27.8 %collective-permute-start.36 = (bf16[128,2048]{1,0:T(8,128)(2,1)S(1)}, bf16[128,2048]{1,0:T(8,128)(2,1)S(1)}, u32[]{:S(2)}, u32[]{:S(2)}) collective-permute-start(bf16[128,2048]{1,0:T(8,128)(2,1)S(1)} %get-tuple-element.306), channel_id=1, source_target_pairs={{0,4},{4,0},{8,12},{12,8},{16,20},{20,16},{24,28},{28,24},{1,5},{5... | collective-permute-start | bytes 1572872 | tf_op jit(solution)/shard_map/ppermute | solution.py:593
  350.8 25.3 %collective-permute-start.40 = (bf16[256,2048]{1,0:T(8,128)(2,1)S(1)}, bf16[256,2048]{1,0:T(8,128)(2,1)S(1)}, u32[]{:S(2)}, u32[]{:S(2)}) collective-permute-start(bf16[256,2048]{1,0:T(8,128)(2,1)S(1)} %get-tuple-element.295), channel_id=1, source_target_pairs={{0,4},{4,0},{8,12},{12,8},{16,20},{20,16},{24,28},{28,24},{1,5},{5... | collective-permute-start | bytes 3145736 | tf_op jit(solution)/shard_map/ppermute | solution.py:593
  351.9 25.1 %collective-permute-start.39 = (bf16[256,2048]{1,0:T(8,128)(2,1)S(1)}, bf16[256,2048]{1,0:T(8,128)(2,1)}, u32[]{:S(2)}, u32[]{:S(2)}) collective-permute-start(bf16[256,2048]{1,0:T(8,128)(2,1)S(1)} %get-tuple-element.296), channel_id=1, source_target_pairs={{0,2},{1,3},{2,0},{3,1},{4,6},{5,7},{6,4},{7,5},{8,10},{9,11},{10,... | collective-permute-start | bytes 3145736 | tf_op jit(solution)/shard_map/ppermute | solution.py:596
  377.1 206.6 %reduce-scatter.8.cloned.1.call-start = ((), (), s32[]{:S(2)}) async-start(), calls=%async_computation.9 | async-start | bytes 5242880 | tf_op jit(solution)/shard_map/reduce_scatter | solution.py:629
  384.2 24.0 %collective-permute-start.42 = (bf16[256,2048]{1,0:T(8,128)(2,1)}, bf16[256,2048]{1,0:T(8,128)(2,1)S(1)}, u32[]{:S(2)}, u32[]{:S(2)}) collective-permute-start(bf16[256,2048]{1,0:T(8,128)(2,1)} %get-tuple-element.224.refs_0_), channel_id=1, source_target_pairs={{0,4},{4,0},{8,12},{12,8},{16,20},{20,16},{24,28},{28,24},{1,5},{5... | collective-permute-start | bytes 3145736 | tf_op jit(solution)/shard_map/ppermute | solution.py:593
  384.5 24.4 %collective-permute-start.41 = (bf16[256,2048]{1,0:T(8,128)(2,1)}, bf16[256,2048]{1,0:T(8,128)(2,1)S(1)}, u32[]{:S(2)}, u32[]{:S(2)}) collective-permute-start(bf16[256,2048]{1,0:T(8,128)(2,1)} %get-tuple-element.224.refs_0_), channel_id=1, source_target_pairs={{0,2},{1,3},{2,0},{3,1},{4,6},{5,7},{6,4},{7,5},{8,10},{9,11},{10,... | collective-permute-start | bytes 3145736 | tf_op jit(solution)/shard_map/ppermute | solution.py:596
  444.9 33.1 %collective-permute-start.54 = (bf16[256,2048]{1,0:T(8,128)(2,1)S(1)}, bf16[256,2048]{1,0:T(8,128)(2,1)S(1)}, u32[]{:S(2)}, u32[]{:S(2)}) collective-permute-start(bf16[256,2048]{1,0:T(8,128)(2,1)S(1)} %add_convert_fusion.3), channel_id=1, source_target_pairs={{0,4},{4,0},{8,12},{12,8},{16,20},{20,16},{24,28},{28,24},{1,5},{5... | collective-permute-start | bytes 3145736 | tf_op jit(solution)/shard_map/ppermute | solution.py:593
  447.2 30.8 %collective-permute-start.53 = (bf16[256,2048]{1,0:T(8,128)(2,1)S(1)}, bf16[256,2048]{1,0:T(8,128)(2,1)S(1)}, u32[]{:S(2)}, u32[]{:S(2)}) collective-permute-start(bf16[256,2048]{1,0:T(8,128)(2,1)S(1)} %add_convert_fusion.4), channel_id=1, source_target_pairs={{0,2},{1,3},{2,0},{3,1},{4,6},{5,7},{6,4},{7,5},{8,10},{9,11},{10,... | collective-permute-start | bytes 3145736 | tf_op jit(solution)/shard_map/ppermute | solution.py:596
  448.2 29.9 %collective-permute-start.55 = (bf16[256,704]{1,0:T(8,128)(2,1)S(1)}, bf16[256,704]{1,0:T(8,128)(2,1)S(1)}, u32[]{:S(2)}, u32[]{:S(2)}) collective-permute-start(bf16[256,704]{1,0:T(8,128)(2,1)S(1)} %get-tuple-element.315), channel_id=1, source_target_pairs={{0,4},{4,0},{8,12},{12,8},{16,20},{20,16},{24,28},{28,24},{1,5},{5... | collective-permute-start | bytes 1081352 | tf_op jit(solution)/shard_map/ppermute | solution.py:593
  (114 other events, 1079.1 us)
Sparse Core Ops, SparseCore 0:
  27.8 64.9 all-gather.4
  95.0 26.5 all-gather.6
  123.8 106.1 all-gather.8
  231.4 61.7 all-gather.10
  310.9 57.5 reduce-scatter.3
  377.1 100.5 reduce-scatter.5
  508.9 74.6 reduce-scatter.7
where the time goes:
time: 620 us; the launch traced here: 612 us
  waiting for transfers between devices  227 us (37%)
  Pallas kernels  202 us (33%)
  starting transfers between devices  55.3 us (9%)
  other arithmetic  49.6 us (8%)
  local copies, waits for them, and re-layouts  42.9 us (7%)
  matrix products  18.5 us (3%)
  between operations  15.6 us (3%)
    ppermute x21, waiting for transfers between devices, to_pair(): return lax.ppermute(v, 'dp', [(i, i ^ 1) for i in range(self.n_dp)])  155 us
    pallas_call x3, Pallas kernels, weight_grad(): pl.pallas_call(over_rows_kernel, grid=(width // tile,), in_specs=specs, o...  44.5 us
    pallas_call x2, Pallas kernels, feed_back(): pl.pallas_call(functools.partial(feed_back_kernel, sends), grid=(2 * send...  39.5 us
    ppermute x16, waiting for transfers between devices, to_side(): return lax.ppermute(v, 'tensor', [(i, i ^ 2) for i in range(self.n_tensor)])  28.6 us
    pallas_call x1, Pallas kernels, attend_back(): pl.pallas_call(attend_back_kernel, grid_spec=pltpu.PrefetchScalarGridSpec...  27.8 us
    pallas_call x2, Pallas kernels, feed(): pl.pallas_call(functools.partial(feed_kernel, count, first), grid=(all_ro...  27.2 us
    ppermute x21, starting transfers between devices, to_pair(): return lax.ppermute(v, 'dp', [(i, i ^ 1) for i in range(self.n_dp)])  24.9 us
    ppermute x27, waiting for transfers between devices, to_core(): return lax.ppermute(v, 'tensor', [(i, i ^ 1) for i in range(self.n_tensor)])  23.4 us
  transfers between devices with their start and end apart: 78, of which 41 were waited for; matrix products, arithmetic and copies ran while one was open for 12% of the time, Pallas kernels for 31%

commit v1 on v0

--- a/solution.py
+++ b/solution.py
@@ -493,6 +493,45 @@
     )(*pieces)
 
 
+def core_sums_kernel(near, other, *refs):
+    own, side, pair = refs
+    for k, out in enumerate((own, side, pair)):
+        out[...] = near[k].astype(F32) + other[k].astype(F32)
+
+
+def core_sums(near, other, step=64):
+    three, rows, width = near.shape
+    blocks = pl.BlockSpec((three, step, width), lambda i: (0, i, 0))
+    return pl.pallas_call(
+        core_sums_kernel,
+        grid=(rows // step,),
+        in_specs=[blocks, blocks],
+        out_specs=[pl.BlockSpec((step, width), lambda i: (i, 0))] * 3,
+        out_shape=[jax.ShapeDtypeStruct((rows, width), F32)] * 3,
+        compiler_params=pltpu.CompilerParams(vmem_limit_bytes=56 * 2**20),
+        cost_estimate=LITTLE,
+        name="core_sums",
+    )(near, other)
+
+
+def add_halves_kernel(side, pair, d1, d2, side_low, pair_low):
+    half = d1.shape[0]
+    side_low[:half] = (side[:half] + d1[...].astype(F32)).astype(BF)
+    side_low[half:] = side[half:].astype(BF)
+    pair_low[:half] = pair[:half].astype(BF)
+    pair_low[half:] = (pair[half:] + d2[...].astype(F32)).astype(BF)
+
+
+def add_halves(side, pair, d1, d2):
+    return pl.pallas_call(
+        add_halves_kernel,
+        out_shape=[jax.ShapeDtypeStruct(side.shape, BF)] * 2,
+        compiler_params=pltpu.CompilerParams(vmem_limit_bytes=56 * 2**20),
+        cost_estimate=LITTLE,
+        name="add_halves",
+    )(side, pair, d1, d2)
+
+
 def norm_kernel(count, *refs):
     terms, (base, gain, shift) = refs[:count], refs[count : count + 3]
     total, unit, inverse, low = refs[-4:]
@@ -655,11 +694,14 @@
     def gather_begin(self, own):
         return self.gather_cores(*self.gather_links(own))
 
-    def gather_end(self, near):
+    def gather_far(self, near):
         side, pair = near[2], near[4]
         half = side.shape[0] // 2
         one, two = lax.optimization_barrier((side[:half], pair[half:]))
-        d1, d2 = self.to_pair(one), self.to_side(two)
+        return self.to_pair(one), self.to_side(two), one, two
+
+    def gather_end(self, near):
+        d1, d2, one, two = self.gather_far(near)
         return (d1, d2, self.to_core(d1), self.to_core(d2)), one, two
 
     def core_sum(self, far, far_sent):
@@ -712,11 +754,12 @@
         return self.scatter_end(self.scatter_middle(self.scatter_begin(*parts)))
 
     def sum_all(self, v):
-        for axis, size in (("tensor", self.n_tensor), ("dp", self.n_dp)):
-            step = 1
+        for axis, size, first in (("tensor", self.n_tensor, 1), ("dp", self.n_dp, 2), ("dp", 2, 1)):
+            length = self.n_tensor if axis == "tensor" else self.n_dp
+            step = first
             while step < size:
                 others = [
-                    lax.ppermute(v, axis, [(i, i ^ (k * step)) for i in range(size)])
+                    lax.ppermute(v, axis, [(i, i ^ (k * step)) for i in range(length)])
                     for k in range(1, 4 if 4 * step <= size else 2)
                 ]
                 v = v + others[0]
@@ -806,10 +849,12 @@
     far, *_ = at.gather_end(near)
     fed_near = feed(near, rows, full_wide, total=tokens)
     cot_links = at.gather_links(after(cotangent, *far))
+    cot_near = at.gather_cores(*all_after(cot_links, fed_near[1]))
+    d1, d2, *halves = at.gather_far(cot_near)
+    far, *_ = lax.optimization_barrier((far, *halves))
     act_two, inner, slope, swish = feed(far, rows, full_wide, fed_near, tokens)
-    cot_near = at.gather_cores(*all_after(cot_links, fed_near[1]))
-    cot_far, *_ = at.gather_end(cot_near)
-    cot_all = assemble(*all_after((*cot_near, *cot_far), inner))
+    d1, d2, inner = lax.optimization_barrier((d1, d2, inner))
+    cot_all = assemble(*cot_near, d1, d2, at.to_core(d1), at.to_core(d2))
     down_grad = weight_grad((cot_all, inner))
     down_total = at.scatter_grad(down_grad)
     d_wide, far_sent, far_kept = feed_back(
@@ -848,20 +893,25 @@
     *fed, down_mine, down_other = fed
     d_qkv = d_qkv.reshape(tokens, 3 * cols)
     sums = sums[0, 0] + sums[1, 0]
-    qkvo_grad = weight_grad((act_one, d_qkv), (d_hidden_all, context_all))
+    wide_sent = at.share_send(after(wide_total, d_qkv))
+    qkvo_grad = weight_grad((act_one, after(d_qkv, *wide_sent[:1])), (d_hidden_all, context_all))
+    qkvo_grad, wide_mine, wide_other = lax.optimization_barrier((qkvo_grad, *wide_sent))
     qkvo_total = at.scatter_grad(qkvo_grad)
-    d_qkv, wide_total = all_after((d_qkv, wide_total), qkvo_grad)
-    begun = at.scatter_begin(*product(d_qkv, full_qkv))
-    *begun, wide_mine, wide_other = lax.optimization_barrier((*begun, *at.share_send(wide_total)))
-    middle = at.scatter_middle(begun)
+    far_kept, far_sent, near_kept, near_sent = product(after(d_qkv, qkvo_grad), full_qkv)
+    far_sum = at.core_sum(far_kept, far_sent)
+    own, side, pair = core_sums(near_kept, at.to_core(near_sent))
+    d1, d2, own, side, pair = lax.optimization_barrier((*at.scatter_far(*far_sum), own, side, pair))
+    middle = (*add_halves(side, pair, d1, d2), own)
     block_output = (hidden + fed[0] + fed[1].astype(F32) + fed[2].astype(F32)).astype(BF)
     d_act_one = at.scatter_end(middle)
     (down_share,) = at.share_grad(*all_after((down_mine, down_other), *middle), 1)
     gate_share, up_share = at.share_grad(*all_after((wide_mine, wide_other), *middle), 2)
+    *d_act_one, down_share, gate_share, up_share, block_output = lax.optimization_barrier(
+        (*d_act_one, down_share, gate_share, up_share, block_output)
+    )
     input_grad, sums_one, _ = norm_back(d_hidden, d_act_one, unit_one, inverse_one, ln1_gain)
-    query_share, key_share, value_share, out_share = at.share_grad(
-        *at.share_send(after(qkvo_total, sums_one)), 4
-    )
+    qkvo_sent = at.share_send(after(qkvo_total, sums_one))
+    query_share, key_share, value_share, out_share = at.share_grad(*qkvo_sent, 4)
 
     query_part, value_part = sums[:cols], sums[2 * cols :]
     key_part = sums[cols : 2 * cols].reshape(heads, HEAD)[:, :ROT].reshape(heads * ROT)
@@ -869,7 +919,10 @@
     value_full = lax.dynamic_update_slice(jnp.zeros(v_bias.shape, F32), value_part, (column,))
     key_full = lax.dynamic_update_slice(jnp.zeros(k_bias.shape, F32), key_part, (key_column,))
     sums = at.sum_all(
-        jnp.concatenate([sums_one[0], sums_one[1], sums_two[0], sums_two[1], query_full, value_full, key_full])
+        after(
+            jnp.concatenate([sums_one[0], sums_one[1], sums_two[0], sums_two[1], query_full, value_full, key_full]),
+            qkvo_sent[0],
+        )
     )
     n = width
     return (

time: 620 us -> 617 us (level)
  waiting for transfers between devices: 227 us -> 213 us
  Pallas kernels: 202 us -> 211 us
  local copies, waits for them, and re-layouts: 42.9 us -> 49.8 us
    ppermute x21, waiting for transfers between devices: 155 us -> 124 us  [to_pair(): return lax.ppermute(v, 'dp', [(i, i ^ 1) for i in range(self.n_dp)])]
    ppermute x7, waiting for transfers between devices: 3.42 us -> 14.3 us  [sum_all(): lax.ppermute(v, axis, [(i, i ^ k * step) for i in range(length)])]
    pallas_call x0 -> x2, Pallas kernels: none -> 9.83 us  [the longest x1 5.87 us: core_sums(): pl.pallas_call(core_sums_kernel, grid=(rows // step,), in_specs=[blocks,...]
    ppermute x16, waiting for transfers between devices: 28.6 us -> 35.1 us  [to_side(): return lax.ppermute(v, 'tensor', [(i, i ^ 2) for i in range(self.n_tensor)])]
    select_n x2 -> x7, other arithmetic: 1.51 us -> 7.85 us  [halves(): jnp.where(self.pair == 0, high, low)]
    unnamed x126 -> x128, local copies, waits for them, and re-layouts: 18.4 us -> 19.7 us
  transfers between devices with their start and end apart: 78 -> 78, of which waited for: 41 -> 47; matrix products, arithmetic and copies ran while one was open for 12% -> 13% of each run, Pallas kernels for 31% -> 33%
where the time goes in v1:
time: 617 us; the launch traced here: 609 us
  waiting for transfers between devices  213 us (35%)
  Pallas kernels  211 us (34%)
  starting transfers between devices  55.4 us (9%)
  local copies, waits for them, and re-layouts  49.8 us (8%)
  other arithmetic  46.1 us (7%)
  matrix products  18.5 us (3%)
  between operations  15.5 us (3%)
    ppermute x21, waiting for transfers between devices, to_pair(): return lax.ppermute(v, 'dp', [(i, i ^ 1) for i in range(self.n_dp)])  124 us
    pallas_call x3, Pallas kernels, weight_grad(): pl.pallas_call(over_rows_kernel, grid=(width // tile,), in_specs=specs, o...  43.7 us
    pallas_call x2, Pallas kernels, feed_back(): pl.pallas_call(functools.partial(feed_back_kernel, sends), grid=(2 * send...  39.5 us
    ppermute x16, waiting for transfers between devices, to_side(): return lax.ppermute(v, 'tensor', [(i, i ^ 2) for i in range(self.n_tensor)])  35.1 us
    pallas_call x1, Pallas kernels, attend_back(): pl.pallas_call(attend_back_kernel, grid_spec=pltpu.PrefetchScalarGridSpec...  27.8 us
    ppermute x21, starting transfers between devices, to_pair(): return lax.ppermute(v, 'dp', [(i, i ^ 1) for i in range(self.n_dp)])  27.4 us
    pallas_call x2, Pallas kernels, feed(): pl.pallas_call(functools.partial(feed_kernel, count, first), grid=(all_ro...  27 us
    ppermute x27, waiting for transfers between devices, to_core(): return lax.ppermute(v, 'tensor', [(i, i ^ 1) for i in range(self.n_tensor)])  23.3 us
  transfers between devices with their start and end apart: 78, of which 47 were waited for; matrix products, arithmetic and copies ran while one was open for 13% of the time, Pallas kernels for 33%

profile of v1, /device:TPU:0, one launch (start us, length us, event | category | flops | bytes accessed | tf_op | source)
XLA Modules:
  0.0 609.4 jit_solution(13701071858473813340)
XLA Ops:
  18.7 7.6 %collective-permute-done.9 = bf16[256,1024]{1,0:T(8,128)(2,1)S(1)} collective-permute-done((bf16[256,1024]{1,0:T(8,128)(2,1)S(1)}, bf16[256,1024]{1,0:T(8,128)(2,1)S(1)}, u32[]{:S(2)}, u32[]{:S(2)}) %collective-permute-start.9) | collective-permute-done | bytes 524320 | tf_op jit(solution)/shard_map/ppermute | solution.py:632
  34.3 18.2 %collective-permute-done.3.refs_4_ = bf16[256,2048]{1,0:T(8,128)(2,1)} collective-permute-done((bf16[256,2048]{1,0:T(8,128)(2,1)}, bf16[256,2048]{1,0:T(8,128)(2,1)}, u32[]{:S(2)}, u32[]{:S(2)}) %collective-permute-start.3) | collective-permute-done | bytes 1048608 | tf_op jit(solution)/shard_map/ppermute | solution.py:632
  64.2 7.1 %collective-permute-done.5.refs_6_ = bf16[128,2048]{1,0:T(8,128)(2,1)S(1)} collective-permute-done((bf16[128,2048]{1,0:T(8,128)(2,1)}, bf16[128,2048]{1,0:T(8,128)(2,1)S(1)}, u32[]{:S(2)}, u32[]{:S(2)}) %collective-permute-start.5) | collective-permute-done | bytes 524320 | tf_op jit(solution)/shard_map/ppermute | solution.py:632
  79.3 13.5 %all-gather.5.cloned.1.call-done.refs_10_ = bf16[2048,768]{1,0:T(8,128)(2,1)} async-done(((bf16[512,768]{1,0:T(8,128)(2,1)}), bf16[2048,768]{1,0:T(8,128)(2,1)}) %all-gather.5.cloned.1.call-update) | async-done | bytes 3145744 | tf_op jit(solution)/shard_map/all_gather | solution.py:665
  92.8 12.8 %project.2 = (bf16[2048,2048]{1,0:T(8,128)(2,1)}, f32[2048,768]{1,0:T(8,128)}) custom-call(bf16[256,2048]{1,0:T(8,128)(2,1)} %get-tuple-element.162.refs_0_, bf16[256,2048]{1,0:T(8,128)(2,1)} %collective-permute-done.refs_1_, bf16[256,2048]{1,0:T(8,128)(2,1)} %collective-permute-done.1.refs_2_, bf16[256,2048]{1,0:T(8,128)(2,1)} %collective-permute-done.2.refs_3_, ...), custom_call_target="tpu_custom_call" | custom-call | tf_op jit(solution)/shard_map/project/pallas_call | solution.py:441
  113.2 12.4 %attend.1 = (bf16[2,4,256,768]{3,2,1,0:T(8,128)(2,1)S(1)}, bf16[2,4,256,256]{3,2,1,0:T(8,128)(2,1)S(1)}, f32[2,4,8,256]{3,2,1,0:T(8,128)S(1)}) custom-call(s32[1]{0:T(128)} %bitcast.me, f32[2,4,256,768]{3,2,1,0:T(8,128)S(1)} %bitcast.112, f32[1,768]{1,0:T(1,128)S(1)} %broadcast_in_dim.33.shift, f32[4,256,128]{2,1,0:T(8,128)S(1)} %concatenate.112.cosine, ...), custom_call_target="tpu_custom_call" | custom-call | tf_op jit(solution)/shard_map/attend/pallas_call | solution.py:117
  144.2 11.0 %collective-permute-done.15 = bf16[128,2048]{1,0:T(8,128)(2,1)S(1)} collective-permute-done((bf16[128,2048]{1,0:T(8,128)(2,1)S(1)}, bf16[128,2048]{1,0:T(8,128)(2,1)S(1)}, u32[]{:S(2)}, u32[]{:S(2)}) %collective-permute-start.15) | collective-permute-done | bytes 524320 | tf_op jit(solution)/shard_map/ppermute | solution.py:635
  161.5 22.1 %collective-permute-done.16.refs_2_ = bf16[256,2048]{1,0:T(8,128)(2,1)S(1)} collective-permute-done((bf16[256,2048]{1,0:T(8,128)(2,1)S(1)}, bf16[256,2048]{1,0:T(8,128)(2,1)S(1)}, u32[]{:S(2)}, u32[]{:S(2)}) %collective-permute-start.16) | collective-permute-done | bytes 1048608 | tf_op jit(solution)/shard_map/ppermute | solution.py:632
  193.0 22.0 %collective-permute-done.18.refs_4_ = bf16[256,2048]{1,0:T(8,128)(2,1)S(1)} collective-permute-done((bf16[256,2048]{1,0:T(8,128)(2,1)}, bf16[256,2048]{1,0:T(8,128)(2,1)S(1)}, u32[]{:S(2)}, u32[]{:S(2)}) %collective-permute-start.18) | collective-permute-done | bytes 1048608 | tf_op jit(solution)/shard_map/ppermute | solution.py:632
  218.0 8.7 %collective-permute-done.19.refs_0_ = bf16[128,2048]{1,0:T(8,128)(2,1)S(1)} collective-permute-done((bf16[128,2048]{1,0:T(8,128)(2,1)S(1)}, bf16[128,2048]{1,0:T(8,128)(2,1)S(1)}, u32[]{:S(2)}, u32[]{:S(2)}) %collective-permute-start.19) | collective-permute-done | bytes 524320 | tf_op jit(solution)/shard_map/ppermute | solution.py:632
  233.1 17.9 %feed.2 = (bf16[2048,2048]{1,0:T(8,128)(2,1)}, bf16[2048,704]{1,0:T(8,128)(2,1)}, bf16[2048,704]{1,0:T(8,128)(2,1)}, bf16[2048,704]{1,0:T(8,128)(2,1)}) custom-call(bf16[256,2048]{1,0:T(8,128)(2,1)} %get-tuple-element.183.refs_0_, bf16[256,2048]{1,0:T(8,128)(2,1)} %copy-done.59, bf16[256,2048]{1,0:T(8,128)(2,1)} %copy-done.53, ...), custom_call_target="tpu_custom_call" | custom-call | flops 8858370048 | bytes 5767168 | tf_op jit(solution)/shard_map/feed/pallas_call | solution.py:290
  258.5 9.2 %feed.3 = (bf16[2048,2048]{1,0:T(8,128)(2,1)}, bf16[2048,704]{1,0:T(8,128)(2,1)}, bf16[2048,704]{1,0:T(8,128)(2,1)}, bf16[2048,704]{1,0:T(8,128)(2,1)}) custom-call(bf16[128,2048]{1,0:T(8,128)(2,1)} %copy-done.35, bf16[128,2048]{1,0:T(8,128)(2,1)} %copy-done.36, ...), custom_call_target="tpu_custom_call", output_to_operand_aliasing={{0}: (5, {}), {1}: (6, {}), {2}: (7, {}), {3}: (8, {})} | custom-call | flops 2952790016 | bytes 5767168 | tf_op jit(solution)/shard_map/feed/pallas_call | solution.py:290
  281.7 10.9 %weight_grad.3 = bf16[2048,704]{1,0:T(8,128)(2,1)} custom-call(bf16[2048,2048]{1,0:T(8,128)(2,1)} %assemble.1.refs_0_, bf16[2048,704]{1,0:T(8,128)(2,1)} %get-tuple-element.228.refs_1_), custom_call_target="tpu_custom_call" | custom-call | tf_op jit(solution)/shard_map/weight_grad/pallas_call | solution.py:389
  293.3 12.7 %feed_back.2 = (bf16[2048,1408]{1,0:T(8,128)(2,1)}, bf16[1,256,2048]{2,1,0:T(8,128)(2,1)}, bf16[1,256,2048]{2,1,0:T(8,128)(2,1)}) custom-call(bf16[2048,2048]{1,0:T(8,128)(2,1)} %assemble.1.refs_0_, bf16[2048,704]{1,0:T(8,128)(2,1)} %all-gather.11.cloned.1.call-done.refs_1_, bf16[2048,1408]{1,0:T(8,128)(2,1)} %all-gather.9.cloned.1.call-done.refs_6_.refs_4_.refs_2_, ...), custom_call_target="tpu_custom_call" | custom-call | flops 4429185024 | bytes 15728640 | tf_op jit(solution)/shard_map/feed_back/pallas_call | solution.py:347
  312.3 26.8 %feed_back.3 = (bf16[2048,1408]{1,0:T(8,128)(2,1)}, bf16[3,256,2048]{2,1,0:T(8,128)(2,1)}, bf16[3,256,2048]{2,1,0:T(8,128)(2,1)}) custom-call(bf16[2048,2048]{1,0:T(8,128)(2,1)} %assemble.1.refs_0_, bf16[2048,704]{1,0:T(8,128)(2,1)} %all-gather.11.cloned.1.call-done.refs_1_, ...), custom_call_target="tpu_custom_call", output_to_operand_aliasing={{0}: (5, {})} | custom-call | flops 13287555072 | bytes 29884416 | tf_op jit(solution)/shard_map/feed_back/pallas_call | solution.py:347
  352.1 18.2 %weight_grad.4 = bf16[2048,1408]{1,0:T(8,128)(2,1)} custom-call(bf16[2048,2048]{1,0:T(8,128)(2,1)} %get-tuple-element.219.refs_0_, bf16[2048,1408]{1,0:T(8,128)(2,1)} %get-tuple-element.221.refs_1_), custom_call_target="tpu_custom_call" | custom-call | tf_op jit(solution)/shard_map/weight_grad/pallas_call | solution.py:389
  374.0 7.0 %norm_back.2 = (f32[256,2048]{1,0:T(8,128)}, f32[2,2048]{1,0:T(2,128)}, bf16[256,2048]{1,0:T(8,128)(2,1)}) custom-call(f32[256,2048]{1,0:T(8,128)} %add_bitcast_fusion.3.refs_0_, bf16[256,2048]{1,0:T(8,128)(2,1)} %collective-permute-done.39.refs_1_, bf16[256,2048]{1,0:T(8,128)(2,1)} %copy-done.29, bf16[256,2048]{1,0:T(8,128)(2,1)} %refs_3_.3, ...), custom_call_target="tpu_custom_call" | custom-call | tf_op jit(solution)/shard_map/norm_back/pallas_call | solution.py:607
  391.1 14.2 %collective-permute-done.42.refs_4_ = bf16[256,2048]{1,0:T(8,128)(2,1)S(1)} collective-permute-done((bf16[256,2048]{1,0:T(8,128)(2,1)}, bf16[256,2048]{1,0:T(8,128)(2,1)S(1)}, u32[]{:S(2)}, u32[]{:S(2)}) %collective-permute-start.42) | collective-permute-done | bytes 1048608 | tf_op jit(solution)/shard_map/ppermute | solution.py:632
  408.5 11.8 %collective-permute-done.46.refs_6_ = bf16[128,2048]{1,0:T(8,128)(2,1)S(1)} collective-permute-done((bf16[128,2048]{1,0:T(8,128)(2,1)S(1)}, bf16[128,2048]{1,0:T(8,128)(2,1)S(1)}, u32[]{:S(2)}, u32[]{:S(2)}) %collective-permute-start.46) | collective-permute-done | bytes 524320 | tf_op jit(solution)/shard_map/ppermute | solution.py:632
  428.4 8.7 %project.3 = (bf16[2048,2048]{1,0:T(8,128)(2,1)}, bf16[2048,256]{1,0:T(8,128)(2,1)}) custom-call(bf16[256,2048]{1,0:T(8,128)(2,1)} %get-tuple-element.232.refs_0_, bf16[256,2048]{1,0:T(8,128)(2,1)} %copy-done.20, bf16[256,2048]{1,0:T(8,128)(2,1)} %copy-done.15, bf16[256,2048]{1,0:T(8,128)(2,1)} %copy-done.19, bf16[256,2048]{1,0:T(8,128)(2,1)} %copy-done.14, ...), custom_call_target="tpu_custom_call" | custom-call | tf_op jit(solution)/shard_map/project/pallas_call | solution.py:441
  446.3 27.8 %attend_back.1 = (bf16[2,4,256,768]{3,2,1,0:T(8,128)(2,1)}, f32[2,1,768]{2,1,0:T(1,128)}) custom-call(s32[1]{0:T(128)} %bitcast.me, bf16[2,4,256,768]{3,2,1,0:T(8,128)(2,1)} %copy-done.4, bf16[2,4,256,256]{3,2,1,0:T(8,128)(2,1)} %copy-done, bf16[2,4,256,256]{3,2,1,0:T(8,128)(2,1)} %bitcast.121, f32[2,4,8,256]{3,2,1,0:T(8,128)} %copy-done.5, ...), custom_call_target="tpu_custom_call" | custom-call | tf_op jit(solution)/shard_map/attend_back/pallas_call | solution.py:207
  478.5 14.6 %weight_grad.5 = bf16[2048,1024]{1,0:T(8,128)(2,1)} custom-call(bf16[2048,2048]{1,0:T(8,128)(2,1)} %get-tuple-element.259.refs_0_, bf16[2048,768]{1,0:T(8,128)(2,1)} %bitcast.115, bf16[2048,2048]{1,0:T(8,128)(2,1)} %get-tuple-element.256.refs_2_, bf16[2048,256]{1,0:T(8,128)(2,1)} %bitcast.111), custom_call_target="tpu_custom_call" | custom-call | tf_op jit(solution)/shard_map/weight_grad/pallas_call | solution.py:389
  545.0 16.8 %collective-permute-done.61.refs_1_ = bf16[256,2048]{1,0:T(8,128)(2,1)S(1)} collective-permute-done((bf16[256,2048]{1,0:T(8,128)(2,1)}, bf16[256,2048]{1,0:T(8,128)(2,1)S(1)}, u32[]{:S(2)}, u32[]{:S(2)}) %collective-permute-start.61) | collective-permute-done | bytes 1048608 | tf_op jit(solution)/shard_map/ppermute | solution.py:635
  588.9 8.3 %collective-permute-done.69 = f32[12800]{0:T(1024)S(1)} collective-permute-done((f32[12800]{0:T(1024)S(1)}, f32[12800]{0:T(1024)S(1)}, u32[]{:S(2)}, u32[]{:S(2)}) %collective-permute-start.69) | collective-permute-done | bytes 51232 | tf_op jit(solution)/shard_map/ppermute | solution.py:762
  (389 shorter events, 253.6 us)
Async XLA Ops:
  7.2 85.7 %all-gather.5.cloned.1.call-start = ((), (), s32[]{:S(2)}) async-start(), calls=%async_computation.3 | async-start | bytes 3932160 | tf_op jit(solution)/shard_map/all_gather | solution.py:665
  27.7 100.2 %all-gather.7.cloned.1.call-start = ((), (), s32[]{:S(2)}) async-start(), calls=%async_computation.4 | async-start | bytes 1310720 | tf_op jit(solution)/shard_map/all_gather | solution.py:665
  27.8 24.7 %collective-permute-start.3 = (bf16[256,2048]{1,0:T(8,128)(2,1)}, bf16[256,2048]{1,0:T(8,128)(2,1)}, u32[]{:S(2)}, u32[]{:S(2)}) collective-permute-start(bf16[256,2048]{1,0:T(8,128)(2,1)} %get-tuple-element.162.refs_0_), channel_id=1, source_target_pairs={{0,4},{4,0},{8,12},{12,8},{16,20},{20,16},{24,28},{28,24},{1,5},{5... | collective-permute-start | bytes 3145736 | tf_op jit(solution)/shard_map/ppermute | solution.py:632
  29.6 24.8 %collective-permute-start.1 = (bf16[256,2048]{1,0:T(8,128)(2,1)}, bf16[256,2048]{1,0:T(8,128)(2,1)}, u32[]{:S(2)}, u32[]{:S(2)}) collective-permute-start(bf16[256,2048]{1,0:T(8,128)(2,1)} %get-tuple-element.162.refs_0_), channel_id=1, source_target_pairs={{0,2},{1,3},{2,0},{3,1},{4,6},{5,7},{6,4},{7,5},{8,10},{9,11},{10,... | collective-permute-start | bytes 3145736 | tf_op jit(solution)/shard_map/ppermute | solution.py:635
  31.1 48.2 %collective-permute-start = (bf16[256,2048]{1,0:T(8,128)(2,1)}, bf16[256,2048]{1,0:T(8,128)(2,1)}, u32[]{:S(2)}, u32[]{:S(2)}) collective-permute-start(bf16[256,2048]{1,0:T(8,128)(2,1)} %get-tuple-element.162.refs_0_), channel_id=1, source_target_pairs={{0,1},{1,0},{2,3},{3,2},{4,5},{5,4},{6,7},{7,6},{8,9},{9,8},{10,11... | collective-permute-start | bytes 3145736 | tf_op jit(solution)/shard_map/ppermute | solution.py:638
  34.3 198.9 %all-gather.9.cloned.1.call-start = ((), (), s32[]{:S(2)}) async-start(), calls=%async_computation.5 | async-start | bytes 7208960 | tf_op jit(solution)/shard_map/all_gather | solution.py:665
  63.7 41.9 %collective-permute-start.10 = (bf16[256,2112]{0,1:T(8,128)(2,1)}, bf16[256,2112]{0,1:T(8,128)(2,1)}, u32[]{:S(2)}, u32[]{:S(2)}) collective-permute-start(bf16[256,2112]{0,1:T(8,128)(2,1)} %copy.49), channel_id=1, source_target_pairs={{0,4},{4,0},{8,12},{12,8},{16,20},{20,16},{24,28},{28,24},{1,5},{5... | collective-permute-start | bytes 3244040 | tf_op jit(solution)/shard_map/ppermute | solution.py:632
  109.1 184.2 %all-gather.11.cloned.1.call-start = ((), (), s32[]{:S(2)}) async-start(), calls=%async_computation.6 | async-start | bytes 3932160 | tf_op jit(solution)/shard_map/all_gather | solution.py:665
  159.5 24.2 %collective-permute-start.16 = (bf16[256,2048]{1,0:T(8,128)(2,1)S(1)}, bf16[256,2048]{1,0:T(8,128)(2,1)S(1)}, u32[]{:S(2)}, u32[]{:S(2)}) collective-permute-start(bf16[256,2048]{1,0:T(8,128)(2,1)S(1)} %get-tuple-element.308), channel_id=1, source_target_pairs={{0,4},{4,0},{8,12},{12,8},{16,20},{20,16},{24,28},{28,24},{1,5},{5... | collective-permute-start | bytes 3145736 | tf_op jit(solution)/shard_map/ppermute | solution.py:632
  191.4 179.0 %reduce-scatter.4.cloned.1.call-start = ((), (), s32[]{:S(2)}) async-start(), calls=%async_computation.7 | async-start | bytes 3932160 | tf_op jit(solution)/shard_map/reduce_scatter | solution.py:668
  229.4 25.2 %collective-permute-start.24 = (bf16[256,2048]{1,0:T(8,128)(2,1)S(1)}, bf16[256,2048]{1,0:T(8,128)(2,1)S(1)}, u32[]{:S(2)}, u32[]{:S(2)}) collective-permute-start(bf16[256,2048]{1,0:T(8,128)(2,1)S(1)} %copy-done.10), channel_id=1, source_target_pairs={{0,4},{4,0},{8,12},{12,8},{16,20},{20,16},{24,28},{28,24},{1,5},{5... | collective-permute-start | bytes 3145736 | tf_op jit(solution)/shard_map/ppermute | solution.py:632
  230.5 24.9 %collective-permute-start.23 = (bf16[256,2048]{1,0:T(8,128)(2,1)S(1)}, bf16[256,2048]{1,0:T(8,128)(2,1)S(1)}, u32[]{:S(2)}, u32[]{:S(2)}) collective-permute-start(bf16[256,2048]{1,0:T(8,128)(2,1)S(1)} %copy-done.10), channel_id=1, source_target_pairs={{0,2},{1,3},{2,0},{3,1},{4,6},{5,7},{6,4},{7,5},{8,10},{9,11},{10,... | collective-permute-start | bytes 3145736 | tf_op jit(solution)/shard_map/ppermute | solution.py:635
  306.0 168.9 %reduce-scatter.6.cloned.1.call-start = ((), (), s32[]{:S(2)}) async-start(), calls=%async_computation.8 | async-start | bytes 7208960 | tf_op jit(solution)/shard_map/reduce_scatter | solution.py:668
  309.3 29.8 %collective-permute-start.37 = (bf16[128,2048]{1,0:T(8,128)(2,1)S(1)}, bf16[128,2048]{1,0:T(8,128)(2,1)S(1)}, u32[]{:S(2)}, u32[]{:S(2)}) collective-permute-start(bf16[128,2048]{1,0:T(8,128)(2,1)S(1)} %get-tuple-element.328), channel_id=1, source_target_pairs={{0,2},{1,3},{2,0},{3,1},{4,6},{5,7},{6,4},{7,5},{8,10},{9,11},{10,... | collective-permute-start | bytes 1572872 | tf_op jit(solution)/shard_map/ppermute | solution.py:635
  310.8 28.3 %collective-permute-start.36 = (bf16[128,2048]{1,0:T(8,128)(2,1)S(1)}, bf16[128,2048]{1,0:T(8,128)(2,1)S(1)}, u32[]{:S(2)}, u32[]{:S(2)}) collective-permute-start(bf16[128,2048]{1,0:T(8,128)(2,1)S(1)} %get-tuple-element.329), channel_id=1, source_target_pairs={{0,4},{4,0},{8,12},{12,8},{16,20},{20,16},{24,28},{28,24},{1,5},{5... | collective-permute-start | bytes 1572872 | tf_op jit(solution)/shard_map/ppermute | solution.py:632
  347.6 25.3 %collective-permute-start.40 = (bf16[256,2048]{1,0:T(8,128)(2,1)S(1)}, bf16[256,2048]{1,0:T(8,128)(2,1)S(1)}, u32[]{:S(2)}, u32[]{:S(2)}) collective-permute-start(bf16[256,2048]{1,0:T(8,128)(2,1)S(1)} %get-tuple-element.318), channel_id=1, source_target_pairs={{0,4},{4,0},{8,12},{12,8},{16,20},{20,16},{24,28},{28,24},{1,5},{5... | collective-permute-start | bytes 3145736 | tf_op jit(solution)/shard_map/ppermute | solution.py:632
  348.3 25.0 %collective-permute-start.39 = (bf16[256,2048]{1,0:T(8,128)(2,1)S(1)}, bf16[256,2048]{1,0:T(8,128)(2,1)}, u32[]{:S(2)}, u32[]{:S(2)}) collective-permute-start(bf16[256,2048]{1,0:T(8,128)(2,1)S(1)} %get-tuple-element.319), channel_id=1, source_target_pairs={{0,2},{1,3},{2,0},{3,1},{4,6},{5,7},{6,4},{7,5},{8,10},{9,11},{10,... | collective-permute-start | bytes 3145736 | tf_op jit(solution)/shard_map/ppermute | solution.py:635
  373.8 198.4 %reduce-scatter.8.cloned.1.call-start = ((), (), s32[]{:S(2)}) async-start(), calls=%async_computation.9 | async-start | bytes 5242880 | tf_op jit(solution)/shard_map/reduce_scatter | solution.py:668
  381.0 24.3 %collective-permute-start.42 = (bf16[256,2048]{1,0:T(8,128)(2,1)}, bf16[256,2048]{1,0:T(8,128)(2,1)S(1)}, u32[]{:S(2)}, u32[]{:S(2)}) collective-permute-start(bf16[256,2048]{1,0:T(8,128)(2,1)} %get-tuple-element.232.refs_0_), channel_id=1, source_target_pairs={{0,4},{4,0},{8,12},{12,8},{16,20},{20,16},{24,28},{28,24},{1,5},{5... | collective-permute-start | bytes 3145736 | tf_op jit(solution)/shard_map/ppermute | solution.py:632
  441.4 32.7 %collective-permute-start.54 = (bf16[256,2048]{1,0:T(8,128)(2,1)S(1)}, bf16[256,2048]{1,0:T(8,128)(2,1)}, u32[]{:S(2)}, u32[]{:S(2)}) collective-permute-start(bf16[256,2048]{1,0:T(8,128)(2,1)S(1)} %add_convert_fusion.1), channel_id=1, source_target_pairs={{0,4},{4,0},{8,12},{12,8},{16,20},{20,16},{24,28},{28,24},{1,5},{5... | collective-permute-start | bytes 3145736 | tf_op jit(solution)/shard_map/ppermute | solution.py:632
  443.3 30.8 %collective-permute-start.53 = (bf16[256,2048]{1,0:T(8,128)(2,1)S(1)}, bf16[256,2048]{1,0:T(8,128)(2,1)}, u32[]{:S(2)}, u32[]{:S(2)}) collective-permute-start(bf16[256,2048]{1,0:T(8,128)(2,1)S(1)} %add_convert_fusion.2), channel_id=1, source_target_pairs={{0,2},{1,3},{2,0},{3,1},{4,6},{5,7},{6,4},{7,5},{8,10},{9,11},{10,... | collective-permute-start | bytes 3145736 | tf_op jit(solution)/shard_map/ppermute | solution.py:635
  444.6 29.5 %collective-permute-start.55 = (bf16[256,704]{1,0:T(8,128)(2,1)S(1)}, bf16[256,704]{1,0:T(8,128)(2,1)S(1)}, u32[]{:S(2)}, u32[]{:S(2)}) collective-permute-start(bf16[256,704]{1,0:T(8,128)(2,1)S(1)} %get-tuple-element.338), channel_id=1, source_target_pairs={{0,4},{4,0},{8,12},{12,8},{16,20},{20,16},{24,28},{28,24},{1,5},{5... | collective-permute-start | bytes 1081352 | tf_op jit(solution)/shard_map/ppermute | solution.py:632
  537.4 24.4 %collective-permute-start.61 = (bf16[256,2048]{1,0:T(8,128)(2,1)}, bf16[256,2048]{1,0:T(8,128)(2,1)S(1)}, u32[]{:S(2)}, u32[]{:S(2)}) collective-permute-start(bf16[256,2048]{1,0:T(8,128)(2,1)} %get-tuple-element.276), channel_id=1, source_target_pairs={{0,2},{1,3},{2,0},{3,1},{4,6},{5,7},{6,4},{7,5},{8,10},{9,11},{10,... | collective-permute-start | bytes 3145736 | tf_op jit(solution)/shard_map/ppermute | solution.py:635
  538.1 24.1 %collective-permute-start.62 = (bf16[256,2048]{1,0:T(8,128)(2,1)}, bf16[256,2048]{1,0:T(8,128)(2,1)S(1)}, u32[]{:S(2)}, u32[]{:S(2)}) collective-permute-start(bf16[256,2048]{1,0:T(8,128)(2,1)} %get-tuple-element.277), channel_id=1, source_target_pairs={{0,4},{4,0},{8,12},{12,8},{16,20},{20,16},{24,28},{28,24},{1,5},{5... | collective-permute-start | bytes 3145736 | tf_op jit(solution)/shard_map/ppermute | solution.py:632
  (115 other events, 999.8 us)
Sparse Core Ops, SparseCore 0:
  27.8 64.9 all-gather.4
  95.0 26.5 all-gather.6
  123.8 106.1 all-gather.8
  231.4 61.7 all-gather.10
  306.1 59.0 reduce-scatter.3
  373.4 100.4 reduce-scatter.5
  494.9 77.2 reduce-scatter.7

commit v2 on v1

--- a/solution.py
+++ b/solution.py
@@ -238,6 +238,7 @@
 def feed_kernel(count, first, *refs):
     pieces, w = refs[:count], refs[count]
     act, inner, slope, swish, held, in_sem, out_sem = refs[-7:]
+    ragged = slope.shape[1] - inner.shape[1]
     step = pl.program_id(0)
     height = pieces[0].shape[0]
     rows, ff = inner.shape
@@ -270,8 +271,11 @@
     sigmoid = 1.0 / (1.0 + jnp.exp(-gate))
     product = gate * sigmoid
     inner[...] = (product * upward).astype(BF)
-    swish[...] = product.astype(BF)
-    slope[...] = (upward * sigmoid * (1.0 + gate * (1.0 - sigmoid))).astype(BF)
+    swish[:, :ff] = product.astype(BF)
+    slope[:, :ff] = (upward * sigmoid * (1.0 + gate * (1.0 - sigmoid))).astype(BF)
+    if ragged:
+        swish[:, ff:] = jnp.zeros((rows, ragged), BF)
+        slope[:, ff:] = jnp.zeros((rows, ragged), BF)
 
     @pl.when(step == count // each - 1)
     def _():
@@ -287,14 +291,16 @@
     first = 0 if earlier is None else total - all_rows
     kept = () if earlier is None else earlier
     block = pl.BlockSpec((rows, ff), lambda i: (i + first // rows, 0))
+    padded = -(-ff // 128) * 128
+    wide_block = pl.BlockSpec((rows, padded), lambda i: (i + first // rows, 0))
     return pl.pallas_call(
         functools.partial(feed_kernel, count, first),
         grid=(all_rows // rows,),
         in_specs=[pl.BlockSpec(memory_space=pltpu.HBM)] * count
         + [pl.BlockSpec(w.shape, lambda i: (0, 0))]
         + [pl.BlockSpec(memory_space=pltpu.HBM)] * len(kept),
-        out_specs=[pl.BlockSpec(memory_space=pltpu.HBM), block, block, block],
-        out_shape=[jax.ShapeDtypeStruct((total, width), BF)] + [jax.ShapeDtypeStruct((total, ff), BF)] * 3,
+        out_specs=[pl.BlockSpec(memory_space=pltpu.HBM), block, wide_block, wide_block],
+        out_shape=[jax.ShapeDtypeStruct((total, n), BF) for n in (width, ff, padded, padded)],
         scratch_shapes=[
             pltpu.VMEM((all_rows, width), BF),
             pltpu.SemaphoreType.DMA((count,)),
@@ -313,9 +319,10 @@
     cot, down, w, slope, swish = refs[:5]
     d_wide, sent, kept = refs[-3:]
     step = pl.program_id(0)
+    ff = w.shape[1] // 2
     d_inner = dot(cot[...], down[...])
-    d_gate = (d_inner * slope[...].astype(F32)).astype(BF)
-    d_upward = (d_inner * swish[...].astype(F32)).astype(BF)
+    d_gate = (d_inner * slope[...].astype(F32)).astype(BF)[:, :ff]
+    d_upward = (d_inner * swish[...].astype(F32)).astype(BF)[:, :ff]
     both = jnp.concatenate([d_gate, d_upward], 1)
     d_wide[...] = both
     result = dot_nt(both, w[...]).astype(BF)
@@ -331,7 +338,7 @@
 
 def feed_back(cot, down, w, slope, swish, slots, rows, earlier=None):
     total, width = cot.shape
-    ff = down.shape[1]
+    ff = w.shape[1] // 2
     sends = len(slots) // 2
     first, stride = slots[0], 2
 
@@ -341,7 +348,7 @@
     def whole_of(v):
         return pl.BlockSpec(v.shape, lambda i: (0, 0))
 
-    narrow = pl.BlockSpec((rows, ff), lambda i: (slot(i), 0))
+    narrow = pl.BlockSpec((rows, slope.shape[1]), lambda i: (slot(i), 0))
     part = jax.ShapeDtypeStruct((sends, rows, width), BF)
     extra = () if earlier is None else (earlier,)
     return pl.pallas_call(
@@ -857,12 +864,13 @@
     cot_all = assemble(*cot_near, d1, d2, at.to_core(d1), at.to_core(d2))
     down_grad = weight_grad((cot_all, inner))
     down_total = at.scatter_grad(down_grad)
+    down_wide = jnp.pad(full_down, ((0, 0), (0, slope.shape[1] - ff)))
     d_wide, far_sent, far_kept = feed_back(
-        after(cot_all, down_grad), full_down, full_wide, slope, swish, FAR, rows
+        after(cot_all, down_grad), down_wide, full_wide, slope, swish, FAR, rows
     )
     far_sum = at.core_sum(far_kept[0], far_sent[0])
     d_wide, near_sent, near_kept = feed_back(
-        after(cot_all, *far_sum), full_down, full_wide, slope, swish, NEAR, rows, d_wide
+        after(cot_all, *far_sum), down_wide, full_wide, slope, swish, NEAR, rows, d_wide
     )
     d1, d2, near_kept, near_sent, d_wide = lax.optimization_barrier(
         (*at.scatter_far(*far_sum), near_kept, near_sent, d_wide)

time: 617 us -> 638 us (1.034)
  waiting for transfers between devices: 213 us -> 232 us
    all_gather x4, waiting for transfers between devices: 14.3 us -> 36.5 us  [gather_piece(): lax.all_gather(piece, 'dp', axis=0, tiled=True, axis_index_groups=self.li...]
    unnamed x128 -> x116, local copies, waits for them, and re-layouts: 19.7 us -> 19.5 us
  transfers between devices with their start and end apart: 78 -> 78, of which waited for: 47 -> 45; matrix products, arithmetic and copies ran while one was open for 13% -> 13% of each run, Pallas kernels for 33% -> 29%
where the time goes in v2:
time: 638 us; the launch traced here: 631 us
  waiting for transfers between devices  232 us (36%)
  Pallas kernels  211 us (33%)
  starting transfers between devices  54.7 us (9%)
  local copies, waits for them, and re-layouts  52.7 us (8%)
  other arithmetic  46 us (7%)
  matrix products  18.5 us (3%)
  between operations  15.5 us (2%)
    ppermute x21, waiting for transfers between devices, to_pair(): return lax.ppermute(v, 'dp', [(i, i ^ 1) for i in range(self.n_dp)])  124 us
    pallas_call x3, Pallas kernels, weight_grad(): pl.pallas_call(over_rows_kernel, grid=(width // tile,), in_specs=specs, o...  43.6 us
    pallas_call x2, Pallas kernels, feed_back(): pl.pallas_call(functools.partial(feed_back_kernel, sends), grid=(2 * send...  39.5 us
    all_gather x4, waiting for transfers between devices, gather_piece(): lax.all_gather(piece, 'dp', axis=0, tiled=True, axis_index_groups=self.li...  36.5 us
    ppermute x16, waiting for transfers between devices, to_side(): return lax.ppermute(v, 'tensor', [(i, i ^ 2) for i in range(self.n_tensor)])  35.3 us
    pallas_call x1, Pallas kernels, attend_back(): pl.pallas_call(attend_back_kernel, grid_spec=pltpu.PrefetchScalarGridSpec...  27.8 us
    pallas_call x2, Pallas kernels, feed(): pl.pallas_call(functools.partial(feed_kernel, count, first), grid=(all_ro...  27.1 us
    ppermute x21, starting transfers between devices, to_pair(): return lax.ppermute(v, 'dp', [(i, i ^ 1) for i in range(self.n_dp)])  26.9 us
  transfers between devices with their start and end apart: 78, of which 45 were waited for; matrix products, arithmetic and copies ran while one was open for 13% of the time, Pallas kernels for 29%

profile of v2, /device:TPU:0, one launch (start us, length us, event | category | flops | bytes accessed | tf_op | source)
XLA Modules:
  0.0 630.5 jit_solution(2662409847898130835)
XLA Ops:
  18.7 7.6 %collective-permute-done.9 = bf16[256,1024]{1,0:T(8,128)(2,1)S(1)} collective-permute-done((bf16[256,1024]{1,0:T(8,128)(2,1)S(1)}, bf16[256,1024]{1,0:T(8,128)(2,1)S(1)}, u32[]{:S(2)}, u32[]{:S(2)}) %collective-permute-start.9) | collective-permute-done | bytes 524320 | tf_op jit(solution)/shard_map/ppermute | solution.py:639
  34.3 18.2 %collective-permute-done.3.refs_4_ = bf16[256,2048]{1,0:T(8,128)(2,1)} collective-permute-done((bf16[256,2048]{1,0:T(8,128)(2,1)}, bf16[256,2048]{1,0:T(8,128)(2,1)}, u32[]{:S(2)}, u32[]{:S(2)}) %collective-permute-start.3) | collective-permute-done | bytes 1048608 | tf_op jit(solution)/shard_map/ppermute | solution.py:639
  64.2 7.1 %collective-permute-done.5.refs_6_ = bf16[128,2048]{1,0:T(8,128)(2,1)S(1)} collective-permute-done((bf16[128,2048]{1,0:T(8,128)(2,1)}, bf16[128,2048]{1,0:T(8,128)(2,1)S(1)}, u32[]{:S(2)}, u32[]{:S(2)}) %collective-permute-start.5) | collective-permute-done | bytes 524320 | tf_op jit(solution)/shard_map/ppermute | solution.py:639
  79.9 12.9 %all-gather.5.cloned.1.call-done.refs_10_ = bf16[2048,768]{1,0:T(8,128)(2,1)} async-done(((bf16[512,768]{1,0:T(8,128)(2,1)}), bf16[2048,768]{1,0:T(8,128)(2,1)}) %all-gather.5.cloned.1.call-update) | async-done | bytes 3145744 | tf_op jit(solution)/shard_map/all_gather | solution.py:672
  92.8 12.8 %project.2 = (bf16[2048,2048]{1,0:T(8,128)(2,1)}, f32[2048,768]{1,0:T(8,128)}) custom-call(bf16[256,2048]{1,0:T(8,128)(2,1)} %get-tuple-element.162.refs_0_, bf16[256,2048]{1,0:T(8,128)(2,1)} %collective-permute-done.refs_1_, bf16[256,2048]{1,0:T(8,128)(2,1)} %collective-permute-done.1.refs_2_, bf16[256,2048]{1,0:T(8,128)(2,1)} %collective-permute-done.2.refs_3_, ...), custom_call_target="tpu_custom_call" | custom-call | tf_op jit(solution)/shard_map/project/pallas_call | solution.py:448
  113.2 12.4 %attend.1 = (bf16[2,4,256,768]{3,2,1,0:T(8,128)(2,1)S(1)}, bf16[2,4,256,256]{3,2,1,0:T(8,128)(2,1)S(1)}, f32[2,4,8,256]{3,2,1,0:T(8,128)S(1)}) custom-call(s32[1]{0:T(128)} %bitcast.me, f32[2,4,256,768]{3,2,1,0:T(8,128)S(1)} %bitcast.112, f32[1,768]{1,0:T(1,128)S(1)} %broadcast_in_dim.33.shift, f32[4,256,128]{2,1,0:T(8,128)S(1)} %concatenate.112.cosine, ...), custom_call_target="tpu_custom_call" | custom-call | tf_op jit(solution)/shard_map/attend/pallas_call | solution.py:117
  144.2 11.0 %collective-permute-done.15 = bf16[128,2048]{1,0:T(8,128)(2,1)S(1)} collective-permute-done((bf16[128,2048]{1,0:T(8,128)(2,1)S(1)}, bf16[128,2048]{1,0:T(8,128)(2,1)S(1)}, u32[]{:S(2)}, u32[]{:S(2)}) %collective-permute-start.15) | collective-permute-done | bytes 524320 | tf_op jit(solution)/shard_map/ppermute | solution.py:642
  161.5 22.1 %collective-permute-done.16.refs_2_ = bf16[256,2048]{1,0:T(8,128)(2,1)S(1)} collective-permute-done((bf16[256,2048]{1,0:T(8,128)(2,1)S(1)}, bf16[256,2048]{1,0:T(8,128)(2,1)S(1)}, u32[]{:S(2)}, u32[]{:S(2)}) %collective-permute-start.16) | collective-permute-done | bytes 1048608 | tf_op jit(solution)/shard_map/ppermute | solution.py:639
  193.0 22.0 %collective-permute-done.18.refs_4_ = bf16[256,2048]{1,0:T(8,128)(2,1)S(1)} collective-permute-done((bf16[256,2048]{1,0:T(8,128)(2,1)}, bf16[256,2048]{1,0:T(8,128)(2,1)S(1)}, u32[]{:S(2)}, u32[]{:S(2)}) %collective-permute-start.18) | collective-permute-done | bytes 1048608 | tf_op jit(solution)/shard_map/ppermute | solution.py:639
  218.0 8.7 %collective-permute-done.19.refs_0_ = bf16[128,2048]{1,0:T(8,128)(2,1)S(1)} collective-permute-done((bf16[128,2048]{1,0:T(8,128)(2,1)S(1)}, bf16[128,2048]{1,0:T(8,128)(2,1)S(1)}, u32[]{:S(2)}, u32[]{:S(2)}) %collective-permute-start.19) | collective-permute-done | bytes 524320 | tf_op jit(solution)/shard_map/ppermute | solution.py:639
  233.1 17.9 %feed.2 = (bf16[2048,2048]{1,0:T(8,128)(2,1)}, bf16[2048,704]{1,0:T(8,128)(2,1)}, bf16[2048,768]{1,0:T(8,128)(2,1)}, bf16[2048,768]{1,0:T(8,128)(2,1)}) custom-call(bf16[256,2048]{1,0:T(8,128)(2,1)} %get-tuple-element.183.refs_0_, bf16[256,2048]{1,0:T(8,128)(2,1)} %copy-done.53, bf16[256,2048]{1,0:T(8,128)(2,1)} %copy-done.47, ...), custom_call_target="tpu_custom_call" | custom-call | flops 8858370048 | bytes 5767168 | tf_op jit(solution)/shard_map/feed/pallas_call | solution.py:296
  257.7 9.2 %feed.3 = (bf16[2048,2048]{1,0:T(8,128)(2,1)}, bf16[2048,704]{1,0:T(8,128)(2,1)}, bf16[2048,768]{1,0:T(8,128)(2,1)}, bf16[2048,768]{1,0:T(8,128)(2,1)}) custom-call(bf16[128,2048]{1,0:T(8,128)(2,1)} %copy-done.33, bf16[128,2048]{1,0:T(8,128)(2,1)} %copy-done.34, ...), custom_call_target="tpu_custom_call", output_to_operand_aliasing={{0}: (5, {}), {1}: (6, {}), {2}: (7, {}), {3}: (8, {})} | custom-call | flops 2952790016 | bytes 5767168 | tf_op jit(solution)/shard_map/feed/pallas_call | solution.py:296
  269.7 23.6 %all-gather.11.cloned.1.call-done = bf16[2048,704]{1,0:T(8,128)(2,1)} async-done(((bf16[512,704]{1,0:T(8,128)(2,1)}), bf16[2048,704]{1,0:T(8,128)(2,1)}) %all-gather.11.cloned.1.call-update) | async-done | bytes 2883600 | tf_op jit(solution)/shard_map/all_gather | solution.py:672
  303.4 10.9 %weight_grad.3 = bf16[2048,704]{1,0:T(8,128)(2,1)} custom-call(bf16[2048,2048]{1,0:T(8,128)(2,1)} %assemble.1.refs_0_, bf16[2048,704]{1,0:T(8,128)(2,1)} %get-tuple-element.228.refs_1_), custom_call_target="tpu_custom_call" | custom-call | tf_op jit(solution)/shard_map/weight_grad/pallas_call | solution.py:396
  314.3 12.7 %feed_back.2 = (bf16[2048,1408]{1,0:T(8,128)(2,1)}, bf16[1,256,2048]{2,1,0:T(8,128)(2,1)}, bf16[1,256,2048]{2,1,0:T(8,128)(2,1)}) custom-call(bf16[2048,2048]{1,0:T(8,128)(2,1)} %assemble.1.refs_0_, bf16[2048,768]{1,0:T(8,128)(2,1)} %pad.15.refs_1_, bf16[2048,1408]{1,0:T(8,128)(2,1)} %all-gather.9.cloned.1.call-done.refs_6_.refs_4_.refs_2_, ...), custom_call_target="tpu_custom_call" | custom-call | flops 4429185024 | bytes 15990784 | tf_op jit(solution)/shard_map/feed_back/pallas_call | solution.py:354
  333.3 26.8 %feed_back.3 = (bf16[2048,1408]{1,0:T(8,128)(2,1)}, bf16[3,256,2048]{2,1,0:T(8,128)(2,1)}, bf16[3,256,2048]{2,1,0:T(8,128)(2,1)}) custom-call(bf16[2048,2048]{1,0:T(8,128)(2,1)} %assemble.1.refs_0_, bf16[2048,768]{1,0:T(8,128)(2,1)} %pad.15.refs_1_, ...), custom_call_target="tpu_custom_call", output_to_operand_aliasing={{0}: (5, {})} | custom-call | flops 13287555072 | bytes 30146560 | tf_op jit(solution)/shard_map/feed_back/pallas_call | solution.py:354
  373.2 18.2 %weight_grad.4 = bf16[2048,1408]{1,0:T(8,128)(2,1)} custom-call(bf16[2048,2048]{1,0:T(8,128)(2,1)} %get-tuple-element.219.refs_0_, bf16[2048,1408]{1,0:T(8,128)(2,1)} %get-tuple-element.221.refs_1_), custom_call_target="tpu_custom_call" | custom-call | tf_op jit(solution)/shard_map/weight_grad/pallas_call | solution.py:396
  412.1 14.3 %collective-permute-done.42.refs_4_ = bf16[256,2048]{1,0:T(8,128)(2,1)S(1)} collective-permute-done((bf16[256,2048]{1,0:T(8,128)(2,1)}, bf16[256,2048]{1,0:T(8,128)(2,1)S(1)}, u32[]{:S(2)}, u32[]{:S(2)}) %collective-permute-start.42) | collective-permute-done | bytes 1048608 | tf_op jit(solution)/shard_map/ppermute | solution.py:639
  431.3 11.1 %collective-permute-done.46.refs_6_ = bf16[128,2048]{1,0:T(8,128)(2,1)S(1)} collective-permute-done((bf16[128,2048]{1,0:T(8,128)(2,1)S(1)}, bf16[128,2048]{1,0:T(8,128)(2,1)S(1)}, u32[]{:S(2)}, u32[]{:S(2)}) %collective-permute-start.46) | collective-permute-done | bytes 524320 | tf_op jit(solution)/shard_map/ppermute | solution.py:639
  450.5 8.7 %project.3 = (bf16[2048,2048]{1,0:T(8,128)(2,1)}, bf16[2048,256]{1,0:T(8,128)(2,1)}) custom-call(bf16[256,2048]{1,0:T(8,128)(2,1)} %get-tuple-element.232.refs_0_, bf16[256,2048]{1,0:T(8,128)(2,1)} %copy-done.21, bf16[256,2048]{1,0:T(8,128)(2,1)} %copy-done.17, bf16[256,2048]{1,0:T(8,128)(2,1)} %copy-done.20, bf16[256,2048]{1,0:T(8,128)(2,1)} %copy-done.15, ...), custom_call_target="tpu_custom_call" | custom-call | tf_op jit(solution)/shard_map/project/pallas_call | solution.py:448
  468.4 27.8 %attend_back.1 = (bf16[2,4,256,768]{3,2,1,0:T(8,128)(2,1)}, f32[2,1,768]{2,1,0:T(1,128)}) custom-call(s32[1]{0:T(128)} %bitcast.me, bf16[2,4,256,768]{3,2,1,0:T(8,128)(2,1)} %copy-done.4, bf16[2,4,256,256]{3,2,1,0:T(8,128)(2,1)} %copy-done, bf16[2,4,256,256]{3,2,1,0:T(8,128)(2,1)} %bitcast.121, f32[2,4,8,256]{3,2,1,0:T(8,128)} %copy-done.5, ...), custom_call_target="tpu_custom_call" | custom-call | tf_op jit(solution)/shard_map/attend_back/pallas_call | solution.py:207
  500.3 14.6 %weight_grad.5 = bf16[2048,1024]{1,0:T(8,128)(2,1)} custom-call(bf16[2048,2048]{1,0:T(8,128)(2,1)} %get-tuple-element.259.refs_0_, bf16[2048,768]{1,0:T(8,128)(2,1)} %bitcast.115, bf16[2048,2048]{1,0:T(8,128)(2,1)} %get-tuple-element.256.refs_2_, bf16[2048,256]{1,0:T(8,128)(2,1)} %bitcast.111), custom_call_target="tpu_custom_call" | custom-call | tf_op jit(solution)/shard_map/weight_grad/pallas_call | solution.py:396
  567.0 16.9 %collective-permute-done.61.refs_1_ = bf16[256,2048]{1,0:T(8,128)(2,1)S(1)} collective-permute-done((bf16[256,2048]{1,0:T(8,128)(2,1)}, bf16[256,2048]{1,0:T(8,128)(2,1)S(1)}, u32[]{:S(2)}, u32[]{:S(2)}) %collective-permute-start.61) | collective-permute-done | bytes 1048608 | tf_op jit(solution)/shard_map/ppermute | solution.py:642
  610.0 8.4 %collective-permute-done.69 = f32[12800]{0:T(1024)S(1)} collective-permute-done((f32[12800]{0:T(1024)S(1)}, f32[12800]{0:T(1024)S(1)}, u32[]{:S(2)}, u32[]{:S(2)}) %collective-permute-start.69) | collective-permute-done | bytes 51232 | tf_op jit(solution)/shard_map/ppermute | solution.py:769
  (378 shorter events, 259.1 us)
Async XLA Ops:
  7.2 85.7 %all-gather.5.cloned.1.call-start = ((), (), s32[]{:S(2)}) async-start(), calls=%async_computation.3 | async-start | bytes 3932160 | tf_op jit(solution)/shard_map/all_gather | solution.py:672
  27.7 100.2 %all-gather.7.cloned.1.call-start = ((), (), s32[]{:S(2)}) async-start(), calls=%async_computation.4 | async-start | bytes 1310720 | tf_op jit(solution)/shard_map/all_gather | solution.py:672
  29.6 24.8 %collective-permute-start.1 = (bf16[256,2048]{1,0:T(8,128)(2,1)}, bf16[256,2048]{1,0:T(8,128)(2,1)}, u32[]{:S(2)}, u32[]{:S(2)}) collective-permute-start(bf16[256,2048]{1,0:T(8,128)(2,1)} %get-tuple-element.162.refs_0_), channel_id=1, source_target_pairs={{0,2},{1,3},{2,0},{3,1},{4,6},{5,7},{6,4},{7,5},{8,10},{9,11},{10,... | collective-permute-start | bytes 3145736 | tf_op jit(solution)/shard_map/ppermute | solution.py:642
  31.1 48.9 %collective-permute-start = (bf16[256,2048]{1,0:T(8,128)(2,1)}, bf16[256,2048]{1,0:T(8,128)(2,1)}, u32[]{:S(2)}, u32[]{:S(2)}) collective-permute-start(bf16[256,2048]{1,0:T(8,128)(2,1)} %get-tuple-element.162.refs_0_), channel_id=1, source_target_pairs={{0,1},{1,0},{2,3},{3,2},{4,5},{5,4},{6,7},{7,6},{8,9},{9,8},{10,11... | collective-permute-start | bytes 3145736 | tf_op jit(solution)/shard_map/ppermute | solution.py:645
  34.3 198.8 %all-gather.9.cloned.1.call-start = ((), (), s32[]{:S(2)}) async-start(), calls=%async_computation.5 | async-start | bytes 7208960 | tf_op jit(solution)/shard_map/all_gather | solution.py:672
  63.7 41.9 %collective-permute-start.10 = (bf16[256,2112]{0,1:T(8,128)(2,1)}, bf16[256,2112]{0,1:T(8,128)(2,1)}, u32[]{:S(2)}, u32[]{:S(2)}) collective-permute-start(bf16[256,2112]{0,1:T(8,128)(2,1)} %copy.49), channel_id=1, source_target_pairs={{0,4},{4,0},{8,12},{12,8},{16,20},{20,16},{24,28},{28,24},{1,5},{5... | collective-permute-start | bytes 3244040 | tf_op jit(solution)/shard_map/ppermute | solution.py:639
  109.1 184.2 %all-gather.11.cloned.1.call-start = ((), (), s32[]{:S(2)}) async-start(), calls=%async_computation.6 | async-start | bytes 3932160 | tf_op jit(solution)/shard_map/all_gather | solution.py:672
  191.4 200.0 %reduce-scatter.4.cloned.1.call-start = ((), (), s32[]{:S(2)}) async-start(), calls=%async_computation.7 | async-start | bytes 3932160 | tf_op jit(solution)/shard_map/reduce_scatter | solution.py:675
  229.4 25.2 %collective-permute-start.24 = (bf16[256,2048]{1,0:T(8,128)(2,1)S(1)}, bf16[256,2048]{1,0:T(8,128)(2,1)S(1)}, u32[]{:S(2)}, u32[]{:S(2)}) collective-permute-start(bf16[256,2048]{1,0:T(8,128)(2,1)S(1)} %copy-done.10), channel_id=1, source_target_pairs={{0,4},{4,0},{8,12},{12,8},{16,20},{20,16},{24,28},{28,24},{1,5},{5... | collective-permute-start | bytes 3145736 | tf_op jit(solution)/shard_map/ppermute | solution.py:639
  230.5 24.9 %collective-permute-start.23 = (bf16[256,2048]{1,0:T(8,128)(2,1)S(1)}, bf16[256,2048]{1,0:T(8,128)(2,1)S(1)}, u32[]{:S(2)}, u32[]{:S(2)}) collective-permute-start(bf16[256,2048]{1,0:T(8,128)(2,1)S(1)} %copy-done.10), channel_id=1, source_target_pairs={{0,2},{1,3},{2,0},{3,1},{4,6},{5,7},{6,4},{7,5},{8,10},{9,11},{10,... | collective-permute-start | bytes 3145736 | tf_op jit(solution)/shard_map/ppermute | solution.py:642
  257.2 39.9 %collective-permute-start.28 = (bf16[256,2048]{1,0:T(8,128)(2,1)S(1)}, bf16[256,2048]{1,0:T(8,128)(2,1)}, u32[]{:S(2)}, u32[]{:S(2)}) collective-permute-start(bf16[256,2048]{1,0:T(8,128)(2,1)S(1)} %copy-done.10), channel_id=1, source_target_pairs={{0,1},{1,0},{2,3},{3,2},{4,5},{5,4},{6,7},{7,6},{8,9},{9,8},{10,11... | collective-permute-start | bytes 3145736 | tf_op jit(solution)/shard_map/ppermute | solution.py:645
  257.2 39.9 %collective-permute-start.29 = (bf16[256,2048]{1,0:T(8,128)(2,1)S(1)}, bf16[256,2048]{1,0:T(8,128)(2,1)}, u32[]{:S(2)}, u32[]{:S(2)}) collective-permute-start(bf16[256,2048]{1,0:T(8,128)(2,1)S(1)} %collective-permute-done.23.refs_2_), channel_id=1, source_target_pairs={{0,1},{1,0},{2,3},{3,2},{4,5},{5,4},{6,7},{7,6},{8,9},{9,8},{10,11... | collective-permute-start | bytes 3145736 | tf_op jit(solution)/shard_map/ppermute | solution.py:645
  257.7 39.4 %collective-permute-start.30 = (bf16[256,2048]{1,0:T(8,128)(2,1)S(1)}, bf16[256,2048]{1,0:T(8,128)(2,1)}, u32[]{:S(2)}, u32[]{:S(2)}) collective-permute-start(bf16[256,2048]{1,0:T(8,128)(2,1)S(1)} %collective-permute-done.24.refs_4_), channel_id=1, source_target_pairs={{0,1},{1,0},{2,3},{3,2},{4,5},{5,4},{6,7},{7,6},{8,9},{9,8},{10,11... | collective-permute-start | bytes 3145736 | tf_op jit(solution)/shard_map/ppermute | solution.py:645
  269.2 27.9 %collective-permute-start.33 = (bf16[128,2048]{1,0:T(8,128)(2,1)}, bf16[128,2048]{1,0:T(8,128)(2,1)}, u32[]{:S(2)}, u32[]{:S(2)}) collective-permute-start(bf16[128,2048]{1,0:T(8,128)(2,1)} %collective-permute-done.31.refs_6_), channel_id=1, source_target_pairs={{0,1},{1,0},{2,3},{3,2},{4,5},{5,4},{6,7},{7,6},{8,9},{9,8},{10,11... | collective-permute-start | bytes 1572872 | tf_op jit(solution)/shard_map/ppermute | solution.py:645
  269.2 27.9 %collective-permute-start.34 = (bf16[128,2048]{1,0:T(8,128)(2,1)}, bf16[128,2048]{1,0:T(8,128)(2,1)}, u32[]{:S(2)}, u32[]{:S(2)}) collective-permute-start(bf16[128,2048]{1,0:T(8,128)(2,1)} %collective-permute-done.32.refs_7_), channel_id=1, source_target_pairs={{0,1},{1,0},{2,3},{3,2},{4,5},{5,4},{6,7},{7,6},{8,9},{9,8},{10,11... | collective-permute-start | bytes 1572872 | tf_op jit(solution)/shard_map/ppermute | solution.py:645
  327.1 169.9 %reduce-scatter.6.cloned.1.call-start = ((), (), s32[]{:S(2)}) async-start(), calls=%async_computation.8 | async-start | bytes 7208960 | tf_op jit(solution)/shard_map/reduce_scatter | solution.py:675
  330.3 29.8 %collective-permute-start.37 = (bf16[128,2048]{1,0:T(8,128)(2,1)S(1)}, bf16[128,2048]{1,0:T(8,128)(2,1)S(1)}, u32[]{:S(2)}, u32[]{:S(2)}) collective-permute-start(bf16[128,2048]{1,0:T(8,128)(2,1)S(1)} %get-tuple-element.328), channel_id=1, source_target_pairs={{0,2},{1,3},{2,0},{3,1},{4,6},{5,7},{6,4},{7,5},{8,10},{9,11},{10,... | collective-permute-start | bytes 1572872 | tf_op jit(solution)/shard_map/ppermute | solution.py:642
  331.8 28.3 %collective-permute-start.36 = (bf16[128,2048]{1,0:T(8,128)(2,1)S(1)}, bf16[128,2048]{1,0:T(8,128)(2,1)S(1)}, u32[]{:S(2)}, u32[]{:S(2)}) collective-permute-start(bf16[128,2048]{1,0:T(8,128)(2,1)S(1)} %get-tuple-element.329), channel_id=1, source_target_pairs={{0,4},{4,0},{8,12},{12,8},{16,20},{20,16},{24,28},{28,24},{1,5},{5... | collective-permute-start | bytes 1572872 | tf_op jit(solution)/shard_map/ppermute | solution.py:639
  368.7 25.3 %collective-permute-start.40 = (bf16[256,2048]{1,0:T(8,128)(2,1)S(1)}, bf16[256,2048]{1,0:T(8,128)(2,1)S(1)}, u32[]{:S(2)}, u32[]{:S(2)}) collective-permute-start(bf16[256,2048]{1,0:T(8,128)(2,1)S(1)} %get-tuple-element.318), channel_id=1, source_target_pairs={{0,4},{4,0},{8,12},{12,8},{16,20},{20,16},{24,28},{28,24},{1,5},{5... | collective-permute-start | bytes 3145736 | tf_op jit(solution)/shard_map/ppermute | solution.py:639
  369.3 25.0 %collective-permute-start.39 = (bf16[256,2048]{1,0:T(8,128)(2,1)S(1)}, bf16[256,2048]{1,0:T(8,128)(2,1)}, u32[]{:S(2)}, u32[]{:S(2)}) collective-permute-start(bf16[256,2048]{1,0:T(8,128)(2,1)S(1)} %get-tuple-element.319), channel_id=1, source_target_pairs={{0,2},{1,3},{2,0},{3,1},{4,6},{5,7},{6,4},{7,5},{8,10},{9,11},{10,... | collective-permute-start | bytes 3145736 | tf_op jit(solution)/shard_map/ppermute | solution.py:642
  394.9 198.3 %reduce-scatter.8.cloned.1.call-start = ((), (), s32[]{:S(2)}) async-start(), calls=%async_computation.9 | async-start | bytes 5242880 | tf_op jit(solution)/shard_map/reduce_scatter | solution.py:675
  463.5 32.7 %collective-permute-start.54 = (bf16[256,2048]{1,0:T(8,128)(2,1)S(1)}, bf16[256,2048]{1,0:T(8,128)(2,1)}, u32[]{:S(2)}, u32[]{:S(2)}) collective-permute-start(bf16[256,2048]{1,0:T(8,128)(2,1)S(1)} %add_convert_fusion.1), channel_id=1, source_target_pairs={{0,4},{4,0},{8,12},{12,8},{16,20},{20,16},{24,28},{28,24},{1,5},{5... | collective-permute-start | bytes 3145736 | tf_op jit(solution)/shard_map/ppermute | solution.py:639
  465.3 30.9 %collective-permute-start.53 = (bf16[256,2048]{1,0:T(8,128)(2,1)S(1)}, bf16[256,2048]{1,0:T(8,128)(2,1)}, u32[]{:S(2)}, u32[]{:S(2)}) collective-permute-start(bf16[256,2048]{1,0:T(8,128)(2,1)S(1)} %add_convert_fusion.2), channel_id=1, source_target_pairs={{0,2},{1,3},{2,0},{3,1},{4,6},{5,7},{6,4},{7,5},{8,10},{9,11},{10,... | collective-permute-start | bytes 3145736 | tf_op jit(solution)/shard_map/ppermute | solution.py:642
  466.7 29.5 %collective-permute-start.55 = (bf16[256,704]{1,0:T(8,128)(2,1)S(1)}, bf16[256,704]{1,0:T(8,128)(2,1)S(1)}, u32[]{:S(2)}, u32[]{:S(2)}) collective-permute-start(bf16[256,704]{1,0:T(8,128)(2,1)S(1)} %get-tuple-element.338), channel_id=1, source_target_pairs={{0,4},{4,0},{8,12},{12,8},{16,20},{20,16},{24,28},{28,24},{1,5},{5... | collective-permute-start | bytes 1081352 | tf_op jit(solution)/shard_map/ppermute | solution.py:639
  (109 other events, 1056.4 us)
Sparse Core Ops, SparseCore 0:
  27.8 64.9 all-gather.4
  95.0 26.5 all-gather.6
  123.8 106.1 all-gather.8
  231.4 61.7 all-gather.10
  327.2 59.0 reduce-scatter.3
  394.4 100.4 reduce-scatter.5
  516.7 76.4 reduce-scatter.7
